TPU v7x, 512 devices: a whole 4x4x16 slice. The times are simulated.
512 devices in a mesh: prow: 32 (over x, y, core), pcol: 16 (over z).
Axes of the slice: x: 4, y: 4, z: 16, core: 2. Of those that a mesh axis runs over, the one named last changes fastest.
Arguments:
- slab: float32 [32768, 4096], P('prow', 'pcol'), may hold values from -6 to 6
- panel: float32 [32768, 256], P('prow', 'pcol'), may hold values from -0.1875 to 0.1875
- pivots: int32 [256], replicated, may hold values from 256 to 32767, as said below
Outputs:
- result: float32 [32768, 4096], P('prow', 'pcol')
Inputs may be any that keep to these rules, and one draw needn't show every extreme that they name: `pivots`: 256 distinct rows, none among the first 256; at most 32 of them lie in the 1024 rows of one process row, and some process row holds exactly 32.
All inputs are finite; a program needn't handle non-finite values.
Results may differ from a plain program's by a relative error of at most 0.00005.
Values sent between devices are 32-bit elements; how exact they have to be, the bound alone decides.
A program may use at most 64 MiB of HBM per device.

v0:
```python
import jax
import jax.numpy as jnp
from jax import lax
from jax.sharding import PartitionSpec as P


def broadcast(value, axis, root):
    mine = lax.axis_index(axis) == root
    return lax.psum(jnp.where(mine, value, jnp.zeros_like(value)), axis)


def solve_block(diag_block, right_side):
    return jax.scipy.linalg.solve_triangular(diag_block, right_side, lower=True, unit_diagonal=True)


def local(slab, panel, pivots):
    row_count = slab.shape[0]
    panel_width = pivots.shape[0]
    row_index = lax.axis_index("prow")
    row_start = row_index * row_count
    held_here = pivots // row_count == row_index
    local_row = jnp.clip(pivots - row_start, 0, row_count - 1)
    picked = jnp.take(slab, local_row, axis=0)
    masked = jnp.where(held_here[:, None], picked, jnp.zeros_like(picked))
    leading, diag_piece = (
        broadcast(slab[:panel_width], "prow", 0),
        broadcast(panel[:panel_width], "prow", 0),
    )
    diag_block = lax.all_gather(diag_piece, "pcol", axis=1, tiled=True)
    pivot_rows = lax.psum(masked, "prow")
    upper_rows = solve_block(diag_block, pivot_rows)
    target_row = jnp.where(held_here, local_row, row_count)
    swapped = slab.at[target_row].set(leading, mode="drop")
    updated = swapped - jnp.dot(
        lax.all_gather(panel, "pcol", axis=1, tiled=True),
        upper_rows,
        precision=lax.Precision.HIGHEST,
        preferred_element_type=jnp.float32,
    )
    top_block = jnp.where(row_index == 0, upper_rows, updated[:panel_width])
    return updated.at[:panel_width].set(top_block)


def solution(mesh):
    return jax.shard_map(
        local,
        mesh=mesh,
        in_specs=(P("prow", "pcol"), P("prow", "pcol"), P()),
        out_specs=P("prow", "pcol"),
        check_vma=False,
    )
```

profile of v0, /device:TPU:32, one launch (start us, length us, event | category | flops | bytes accessed | tf_op | source)
XLA Modules:
  0.0 216.6 jit_solution(5361861571704352834)
XLA Ops:
  7.4 0.0 all-reduce.3.cloned.1.call-start
  7.4 1.2 copy.24
  8.6 0.0 copy-start.1
  8.6 0.7 copy-done.1
  9.3 1.0 gather_fusion
  10.3 0.7 slice_select_fusion.1
  11.0 0.8 select_select_fusion
  11.9 0.0 all-reduce.3.cloned.1.call-update
  11.9 0.0 all-gather.2.cloned.1.call-start
  11.9 0.5 all-gather.2.cloned.1.call-update
  12.5 0.7 slice_select_fusion.2
  13.2 128.4 %psum.22 = f32[256,16]{0,1:T(8,128)S(1)} all-reduce(f32[256,16]{0,1:T(8,128)S(1)} %slice_select_fusion.2), channel_id=1, replica_groups=mesh['prow'=32,'pcol'=16] {'prow'}, use_global_device_ids=true, to_apply=%region_2.3 | all-reduce | flops 4096 | bytes 32768 | tf_op jit(solution)/shard_map/psum | solution.py:9
  141.6 34.6 %all_gather.6 = f32[256,256]{0,1:T(8,128)S(1)} all-gather(f32[256,16]{0,1:T(8,128)S(1)} %psum.22), channel_id=1, replica_groups=mesh['prow'=32,'pcol'=16] {'pcol'}, dimensions={1}, use_global_device_ids=true | all-gather | bytes 278528 | tf_op jit(solution)/shard_map/all_gather | solution.py:29
  176.2 0.1 copy.8
  176.4 0.1 convert_add_fusion
  176.5 0.1 triangular_solve.72
  176.6 4.0 %while.2 = (s32[]{:T(128)}, f32[256,256]{1,0:T(8,128)S(1)}, s32[2,2]{1,0:T(2,128)S(1)}, f32[2,128,128]{2,1,0:T(8,128)S(1)}, s32[]{:T(128)}) while((s32[]{:T(128)}, f32[256,256]{1,0:T(8,128)S(1)}, s32[2,2]{1,0:T(2,128)S(1)}, f32[2,128,128]{2,1,0:T(8,128)S(1)}, s32[]{:T(128)}) %tuple.25), condition=%wide.while_cond.1, body=%wide.while_body.1.sunk | while | flops 2 | bytes 131181 | solution.py:13
  176.6 0.6 fusion.14
  177.2 1.3 bitcast_dynamic-update-slice_fusion.2
  178.6 0.6 fusion.14
  179.2 1.3 bitcast_dynamic-update-slice_fusion.2
  180.5 19.7 %custom-call.4 = f32[2,128,128]{1,2,0:T(8,128)S(1)} custom-call(f32[2,128,128]{2,1,0:T(8,128)S(1)} %get-tuple-element.24), custom_call_target="InvertDiagBlocksLowerTriangular" | custom-call | tf_op jit(solution)/shard_map/jit(_solve_triangular)/triangular_solve | solution.py:13
  200.2 0.0 all-reduce.3.cloned.1.call-done
  200.3 0.0 copy-start
  200.3 2.2 %scatter_fusion = f32[1024,256]{1,0:T(8,128)S(1)} fusion(f32[1024,256]{1,0:T(8,128)S(1)} %copy.24, s32[256]{0:T(256)S(1)} %get-tuple-element.37, f32[256,256]{1,0:T(8,128)} %get-tuple-element.33), kind=kCustom, calls=%fused_computation.1 | custom fusion | bytes 787456 | tf_op jit(solution)/shard_map/scatter | solution.py:33
  202.5 0.0 copy-done
  202.5 0.3 fusion.2
  202.8 0.3 convolution_subtract_fusion
  203.1 0.3 fusion.5
  203.4 0.0 all-gather.2.cloned.1.call-done
  203.5 4.0 %fusion = f32[1024,256]{1,0:T(8,128)} fusion(f32[1024,256]{1,0:T(8,128)S(1)} %scatter_fusion, f32[1024,256]{0,1:T(8,128)} %all-gather.2.cloned.1.call-done, f32[128,256]{1,0:T(8,128)S(1)} %fusion.5, f32[128,256]{1,0:T(8,128)S(1)} %fusion.2), kind=kOutput, calls=%fused_computation.5 | convolution fusion | flops 805634048 | bytes 3407872 | tf_op jit(solution)/shard_map/dot_general | solution.py:34
  207.5 1.7 fusion.1
  (8 shorter events, 0.1 us)
Async XLA Ops:
  7.4 192.9 %all-reduce.3.cloned.1.call-start = ((), (), s32[]{:S(2)}) async-start(), calls=%async_computation.1 | async-start | bytes 1048576 | tf_op jit(solution)/shard_map/psum | solution.py:9
  8.6 0.7 copy-start.1
  11.9 191.6 %all-gather.2.cloned.1.call-start = ((), (), s32[]{:S(2)}) async-start(), calls=%async_computation | async-start | bytes 1114112 | tf_op jit(solution)/shard_map/all_gather | solution.py:35
  200.3 2.3 %copy-start = (f32[256,256]{1,0:T(8,128)S(1)}, f32[256,256]{1,0:T(8,128)}, u32[]{:S(2)}) copy-start(f32[256,256]{1,0:T(8,128)} %get-tuple-element.34) | copy-start | bytes 786436
Sparse Core Ops, SparseCore 0:
  12.0 138.7 all-reduce.2
Sparse Core Ops, SparseCore 1:
  14.6 75.2 all-gather.1
where the time goes:
time: 217 us
  blocking collectives  163 us (75%)
  other arithmetic  23.8 us (11%)
  between operations  15 us (7%)
  local copies, waits for them, and re-layouts  9.24 us (4%)
  matrix products  4.89 us (2%)
    psum x1, blocking collectives, broadcast(): return lax.psum(jnp.where(mine, value, jnp.zeros_like(value)), axis)  128 us
    all_gather x1, blocking collectives, local(): diag_block = lax.all_gather(diag_piece, 'pcol', axis=1, tiled=True)  34.6 us
    another operation x4, other arithmetic, solve_block(): jax.scipy.linalg.solve_triangular(diag_block, right_side, lower=True, uni...  19.8 us
  transfers between devices with their start and end apart: 2, of which 0 were waited for; matrix products, arithmetic and copies ran while one was open for 13% of the time, Pallas kernels for 0%

commit v1 on v0

v1 whole, which is shorter than its diff:
```python
import jax
import jax.numpy as jnp
from jax import lax
from jax.experimental import pallas as pl
from jax.experimental.pallas import tpu as pltpu
from jax.sharding import PartitionSpec as P

MESH = pl.DeviceIdType.MESH
F32 = jnp.float32
BF16 = jnp.bfloat16
NB = 256
ROWS = 1024
COLS = 256
NZ = 16
CHIPS = 16
HALF = 128
WIDTH = 16
STEPS = 8


def exchange_kernel(
    piv, slab, panel, pt, gathered, diag,
    rows, masked, from_sibling, landed, mine, lead_in, piece, piece_in, column,
    local_sem, ring_send, ring_recv, a_send, a_recv, b_send, b_recv, c_send, c_recv,
    lead_send, lead_recv, p_send, p_recv, rs_send, rs_recv, ag_send, ag_recv, sib_send, sib_recv,
):
    p = lax.axis_index("prow")
    z = lax.axis_index("pcol")
    chip = p // 2
    core = p % 2
    sibling = 2 * chip + 1 - core
    is_root = p == 0

    def near(o):
        return 2 * ((chip + o) % CHIPS) + core

    def above(o):
        return (z + o) % NZ

    barrier = pltpu.get_barrier_semaphore()

    def greet(device):
        pl.semaphore_signal(barrier, inc=1, device_id=device, device_id_type=MESH)

    def greet_planar(o, carry):
        greet((near(o), z))
        return carry

    def greet_column(o, carry):
        greet((p, above(o)))
        return carry

    lax.fori_loop(1, NZ, greet_column, 0)
    lax.fori_loop(1, CHIPS, greet_planar, 0)
    greet((sibling, z))

    def far(o):
        return (2 * o + 1, z)

    @pl.when(is_root)
    def _():
        def body(o, carry):
            greet(far(o))
            return carry
        lax.fori_loop(1, CHIPS, body, 0)

    @pl.when((core == 1) & (chip > 0))
    def _():
        greet((0, z))

    panel_copy = pltpu.make_async_copy(panel, pt.at[z], local_sem.at[0])
    slab_copy = pltpu.make_async_copy(slab, rows, local_sem.at[1])
    panel_copy.start()
    slab_copy.start()
    panel_copy.wait()
    for k in range(WIDTH):
        for h in range(2):
            piece[2 * k + h] = pt[z, k : k + 1, h * HALF : (h + 1) * HALF]
    slab_copy.wait()

    row_start = p * ROWS

    def pick(k, carry):
        local = piv[k] - row_start
        held = (local >= 0) & (local < ROWS)
        row = rows[pl.ds(jnp.clip(local, 0, ROWS - 1), 1), :]
        row = jnp.where(held, row, 0.0)
        masked[0, pl.ds(k, 1), :] = row[:, :HALF]
        masked[1, pl.ds(k, 1), :] = row[:, HALF:]
        return carry

    lax.fori_loop(0, NB, pick, 0, unroll=8)

    extra = jnp.where(is_root, 15, jnp.where((core == 1) & (chip > 0), 1, 0))
    pl.semaphore_wait(barrier, 31 + extra)

    def remote(src, dst, send, recv, device):
        return pltpu.make_async_remote_copy(
            src_ref=src, dst_ref=dst, send_sem=send, recv_sem=recv, device_id=device, device_id_type=MESH
        )

    def ring_copy(direction, step, half):
        block = (z - direction * step) % NZ
        part = pt.at[block, pl.ds(8 * half, 8)]
        d = (direction + 1) // 2
        return remote(
            part, part, ring_send.at[d, step, half], ring_recv.at[d, step, half], (p, (z + direction) % NZ)
        )

    def ring_uses(direction, step, half):
        if step < STEPS - 1:
            return True
        return step == STEPS - 1 and half == (0 if direction == 1 else 1)

    ring_legs = [(d, h) for h in range(2) for d in (1, -1)]

    def ring_step(step):
        for d, h in ring_legs:
            if step > 0 and ring_uses(d, step - 1, h):
                ring_copy(d, step - 1, h).wait_recv()
            if ring_uses(d, step, h):
                ring_copy(d, step, h).start()

    def a_copy(target):
        return remote(piece.at[target], piece_in.at[z], a_send.at[target], a_recv, (target, z))

    def lead_copy(target):
        t_chip, t_core = target // 2, target % 2
        src = rows.at[pl.ds(t_chip * 16, 16), pl.ds(pl.multiple_of(t_core * HALF, HALF), HALF)]
        return remote(src, lead_in, lead_send.at[target], lead_recv, (target, z))

    @pl.when(is_root)
    def _():
        def body(t, carry):
            a_copy(t).start()
            return carry
        lax.fori_loop(1, 2 * CHIPS, body, 0)
        piece_in[z] = piece[0]

    sib_p = remote(masked.at[1 - core], from_sibling, p_send, p_recv, (sibling, z))
    sib_p.start()

    ring_step(0)

    @pl.when(is_root)
    def _():
        def body(t, carry):
            lead_copy(t).start()
            return carry
        lax.fori_loop(1, 2 * CHIPS, body, 0)
        lead_in[...] = rows[0:16, 0:HALF]

    sib_p.wait_recv()
    masked[2] = masked[core] + from_sibling[...]

    def rs_copy(o):
        t_chip = (chip + o) % CHIPS
        return remote(
            masked.at[2, pl.ds(t_chip * 16, 16)], landed.at[o], rs_send.at[o], rs_recv.at[o], (near(o), z)
        )

    def loop(first, last, act):
        def body(o, carry):
            act(o)
            return carry
        lax.fori_loop(first, last, body, 0)

    loop(1, CHIPS, lambda o: rs_copy(o).start())

    ring_step(1)

    @pl.when(p > 0)
    def _():
        a_copy(p).wait_recv()

    def b_copy(o):
        return remote(piece_in.at[z], piece_in.at[z], b_send.at[o], b_recv.at[o], (p, above(o)))

    loop(1, NZ, lambda o: b_copy(o).start())

    ring_step(2)

    loop(1, CHIPS, lambda o: rs_copy(o).wait_recv())

    @pl.when(p > 0)
    def _():
        lead_copy(p).wait_recv()

    total = masked[2, pl.ds(chip * 16, 16)]
    for o in range(1, CHIPS):
        total = total + landed[o]
    mine[0] = total
    mine[1] = lead_in[...]
    gathered[core, chip] = mine[...]

    def ag_copy(o):
        return remote(mine, gathered.at[core, chip], ag_send.at[o], ag_recv.at[o], (near(o), z))

    loop(1, CHIPS, lambda o: ag_copy(o).start())

    ring_step(3)

    loop(1, NZ, lambda o: b_copy(o).wait_recv())
    for k in range(NZ):
        column[k : k + 1, :] = piece_in[k]
    diag[core, chip] = column[...]

    def c_copy(o):
        return remote(column, diag.at[core, chip], c_send.at[o], c_recv.at[o], (near(o), z))

    loop(1, CHIPS, lambda o: c_copy(o).start())

    ring_step(4)

    loop(1, CHIPS, lambda o: ag_copy(o).wait_recv())
    sib_g = remote(gathered.at[core], gathered.at[core], sib_send.at[0], sib_recv.at[0], (sibling, z))
    sib_g.start()

    ring_step(5)

    loop(1, CHIPS, lambda o: c_copy(o).wait_recv())
    sib_d = remote(diag.at[core], diag.at[core], sib_send.at[1], sib_recv.at[1], (sibling, z))
    sib_d.start()

    ring_step(6)
    ring_step(7)
    ring_step(8)

    sib_g.wait_recv()
    sib_d.wait_recv()

    sib_p.wait_send()
    sib_g.wait_send()
    sib_d.wait_send()
    loop(1, CHIPS, lambda o: rs_copy(o).wait_send())
    loop(1, CHIPS, lambda o: ag_copy(o).wait_send())
    loop(1, CHIPS, lambda o: c_copy(o).wait_send())
    loop(1, NZ, lambda o: b_copy(o).wait_send())
    for step in range(STEPS):
        for d, h in ring_legs:
            if ring_uses(d, step, h):
                ring_copy(d, step, h).wait_send()

    @pl.when(is_root)
    def _():
        def body(t, carry):
            a_copy(t).wait_send()
            lead_copy(t).wait_send()
            return carry
        lax.fori_loop(1, 2 * CHIPS, body, 0)


def exchange(slab, panel_t, pivots):
    dma = pltpu.SemaphoreType.DMA
    return pl.pallas_call(
        exchange_kernel,
        name="exchange",
        out_shape=(
            jax.ShapeDtypeStruct((NZ, WIDTH, ROWS), F32),
            jax.ShapeDtypeStruct((2, CHIPS, 2, 16, HALF), F32),
            jax.ShapeDtypeStruct((2, CHIPS, NZ, HALF), F32),
        ),
        in_specs=[
            pl.BlockSpec(memory_space=pltpu.SMEM),
            pl.BlockSpec(memory_space=pl.ANY),
            pl.BlockSpec(memory_space=pl.ANY),
        ],
        out_specs=(pl.BlockSpec(memory_space=pltpu.VMEM),) * 3,
        scratch_shapes=[
            pltpu.VMEM((ROWS, COLS), F32),
            pltpu.VMEM((3, NB, HALF), F32),
            pltpu.VMEM((NB, HALF), F32),
            pltpu.VMEM((CHIPS, 16, HALF), F32),
            pltpu.VMEM((2, 16, HALF), F32),
            pltpu.VMEM((16, HALF), F32),
            pltpu.VMEM((2 * CHIPS, 1, HALF), F32),
            pltpu.VMEM((NZ, 1, HALF), F32),
            pltpu.VMEM((NZ, HALF), F32),
            dma((2,)),
            dma((2, STEPS, 2)), dma((2, STEPS, 2)),
            dma((2 * CHIPS,)), dma,
            dma((NZ,)), dma((NZ,)),
            dma((CHIPS,)), dma((CHIPS,)),
            dma((2 * CHIPS,)), dma,
            dma, dma,
            dma((CHIPS,)), dma((CHIPS,)),
            dma((CHIPS,)), dma((CHIPS,)),
            dma((2,)), dma((2,)),
        ],
        compiler_params=pltpu.CompilerParams(
            collective_id=0, has_side_effects=True, vmem_limit_bytes=24 * 1024 * 1024
        ),
    )(pivots, slab, panel_t)


def split(a):
    high = a.astype(BF16)
    return high, (a - high.astype(F32)).astype(BF16)


def dot3(a, b, dims=(((1,), (0,)), ((), ()))):
    def one(x, y):
        return lax.dot_general(x, y, dims, preferred_element_type=F32)

    return one(a[0], b[0]) + (one(a[0], b[1]) + one(a[1], b[0]))


def invert(lower):
    row = lax.broadcasted_iota(jnp.int32, (NB, NB), 0)
    col = lax.broadcasted_iota(jnp.int32, (NB, NB), 1)
    base = 16
    blocks = NB // base
    on_diag = (row // base) == (col // base)
    packed = jnp.sum(jnp.where(on_diag, lower, 0.0).reshape(blocks, base, NB), axis=0)
    small_row = lax.broadcasted_iota(jnp.int32, (base, NB), 0)
    small_col = lax.broadcasted_iota(jnp.int32, (base, NB), 1)
    lane = lax.broadcasted_iota(jnp.int32, (base, HALF), 1)
    inverse = jnp.where(small_row == small_col % base, 1.0, 0.0)
    for k in range(base - 1):
        index = (lane // base) * base + k
        factor = jnp.concatenate(
            [jnp.take_along_axis(packed[:, h * HALF : (h + 1) * HALF], index, axis=1) for h in range(2)], axis=1
        )
        inverse = inverse - factor * inverse[k : k + 1, :]
    inverse = jnp.where(on_diag, jnp.concatenate([inverse] * blocks, axis=0), 0.0)
    size = base
    while size < NB:
        same = (row // (2 * size)) == (col // (2 * size))
        below = same & ((row // size) % 2 == 1) & ((col // size) % 2 == 0)
        corner = jnp.where(below, lower, 0.0)
        parts = split(inverse)
        inverse = inverse - dot3(parts, split(dot3(split(corner), parts)))
        size *= 2
    return inverse


def update_kernel(piv, slab, pt, gathered, diag, out, rows, leading, upper_t, result, load_sem, store_sem):
    p = lax.axis_index("prow")
    load = pltpu.make_async_copy(slab, rows.at[pl.ds(0, ROWS)], load_sem)
    load.start()

    for h in range(2):
        for z in range(NZ):
            upper_t[z * 16 : (z + 1) * 16, h * HALF : (h + 1) * HALF] = diag[h, pl.ds(z, 16, stride=NZ), :]
    row = lax.broadcasted_iota(jnp.int32, (NB, NB), 0)
    col = lax.broadcasted_iota(jnp.int32, (NB, NB), 1)
    lower = jnp.where(row > col, upper_t[...].T, 0.0)
    inverse = invert(lower)
    pivot_rows = jnp.concatenate([gathered[h, :, 0].reshape(NB, HALF) for h in range(2)], axis=1)
    upper = dot3(split(inverse), split(pivot_rows))
    upper_parts = split(upper)

    load.wait()

    def swap(k, carry):
        local = piv[k] - p * ROWS
        held = (local >= 0) & (local < ROWS)
        target = jnp.where(held, local, ROWS)
        rows[pl.ds(target, 1), :] = leading[pl.ds(k, 1), :]
        return carry

    for h in range(2):
        leading[:, h * HALF : (h + 1) * HALF] = gathered[h, :, 1].reshape(NB, HALF)
    lax.fori_loop(0, NB, swap, 0, unroll=8)

    chunk = 256
    for n in range(ROWS // chunk):
        block = pt[:, n * chunk : (n + 1) * chunk]
        product = dot3(split(block), upper_parts, (((0,), (0,)), ((), ())))
        value = rows[n * chunk : (n + 1) * chunk, :] - product
        if n == 0:
            value = jnp.where(p == 0, upper, value)
        result[n * chunk : (n + 1) * chunk, :] = value
        pltpu.make_async_copy(
            result.at[pl.ds(n * chunk, chunk)], out.at[pl.ds(n * chunk, chunk)], store_sem.at[n]
        ).start()
    for n in range(ROWS // chunk):
        pltpu.make_async_copy(
            result.at[pl.ds(n * chunk, chunk)], out.at[pl.ds(n * chunk, chunk)], store_sem.at[n]
        ).wait()


def finish(slab, pivots, pt, gathered, diag):
    vmem = pl.BlockSpec(memory_space=pltpu.VMEM)
    hbm = pl.BlockSpec(memory_space=pl.ANY)
    return pl.pallas_call(
        update_kernel,
        name="finish",
        out_shape=jax.ShapeDtypeStruct((ROWS, COLS), F32),
        in_specs=[pl.BlockSpec(memory_space=pltpu.SMEM), hbm, vmem, vmem, vmem],
        out_specs=hbm,
        scratch_shapes=[
            pltpu.VMEM((ROWS + 8, COLS), F32),
            pltpu.VMEM((NB, COLS), F32),
            pltpu.VMEM((NB, NB), F32),
            pltpu.VMEM((ROWS, COLS), F32),
            pltpu.SemaphoreType.DMA,
            pltpu.SemaphoreType.DMA((4,)),
        ],
        compiler_params=pltpu.CompilerParams(vmem_limit_bytes=32 * 1024 * 1024),
    )(pivots, slab, pt.reshape(NZ * WIDTH, ROWS), gathered, diag.reshape(2, NB, HALF))


def local(slab, panel, pivots):
    pt, gathered, diag = exchange(slab, panel.T, pivots)
    return finish(slab, pivots, pt, gathered, diag)


def solution(mesh):
    return jax.shard_map(
        local,
        mesh=mesh,
        in_specs=(P("prow", "pcol"), P("prow", "pcol"), P()),
        out_specs=P("prow", "pcol"),
        check_vma=False,
    )
```

time: 217 us -> 54.2 us (0.25)
  the two profiles are of different devices: /device:TPU:32 before, /device:TPU:18 now
where the time goes in v1:
time: 54.2 us; the launch traced here: 53.9 us
  Pallas kernels  51.2 us (94%)
  local copies, waits for them, and re-layouts  2.75 us (5%)
    pallas_call x1, Pallas kernels, exchange(): pl.pallas_call(exchange_kernel, name='exchange', out_shape=(jax.ShapeDtyp...  44.7 us
    pallas_call x1, Pallas kernels, finish(): pl.pallas_call(update_kernel, name='finish', out_shape=jax.ShapeDtypeStru...  6.53 us
    unnamed x8, local copies, waits for them, and re-layouts  2.75 us

profile of v1, /device:TPU:18, one launch (start us, length us, event | category | flops | bytes accessed | tf_op | source)
XLA Modules:
  0.0 53.9 jit_solution(15259728347974722938)
XLA Ops:
  0.0 0.0 copy-start.3
  0.0 0.7 %copy-done.3 = s32[256]{0:T(256)S(1)} copy-done((s32[256]{0:T(256)S(1)}, s32[256]{0:T(256)}, u32[]{:S(2)}) %copy-start.3) | copy-done | bytes 1048
  0.7 0.0 copy-start
  0.7 1.2 %copy-done = f32[1024,256]{1,0:T(8,128)S(1)} copy-done((f32[1024,256]{1,0:T(8,128)S(1)}, f32[1024,256]{1,0:T(8,128)}, u32[]{:S(2)}) %copy-start) | copy-done | bytes 1048600
  1.9 0.0 copy-start.2
  1.9 0.8 %copy-done.2 = f32[1024,16]{0,1:T(8,128)S(1)} copy-done((f32[1024,16]{0,1:T(8,128)S(1)}, f32[1024,16]{0,1:T(8,128)}, u32[]{:S(2)}) %copy-start.2) | copy-done | bytes 65560
  2.7 0.0 copy-start.1
  2.7 44.7 %exchange.1 = (f32[16,16,1024]{2,1,0:T(8,128)S(1)}, f32[2,16,2,16,128]{4,3,2,1,0:T(8,128)S(1)}, f32[2,16,16,128]{3,2,1,0:T(8,128)S(1)}) custom-call(s32[256]{0:T(256)S(1)} %copy-done.3, f32[1024,256]{1,0:T(8,128)S(1)} %copy-done, f32[16,1024]{1,0:T(8,128)S(1)} %bitcast.5), custom_call_target="tpu_custom_call" | custom-call | tf_op jit(solution)/shard_map/exchange/pallas_call | solution.py:255
  47.4 0.0 copy-done.1
  47.4 6.5 %finish.1 = f32[1024,256]{1,0:T(8,128)} custom-call(s32[256]{0:T(256)S(1)} %copy-done.3, f32[1024,256]{1,0:T(8,128)S(1)} %copy-done.1, f32[256,1024]{1,0:T(8,128)S(1)} %bitcast.3, f32[2,16,2,16,128]{4,3,2,1,0:T(8,128)S(1)} %get-tuple-element.9.gathered, f32[2,256,128]{2,1,0:T(8,128)S(1)} %bitcast.4), custom_call_target="tpu_custom_call" | custom-call | tf_op jit(solution)/shard_map/finish/pallas_call | solution.py:386
Async XLA Ops:
  0.0 0.7 %copy-start.3 = (s32[256]{0:T(256)S(1)}, s32[256]{0:T(256)}, u32[]{:S(2)}) copy-start(s32[256]{0:T(256)} %piv.3) | copy-start | bytes 3076
  0.7 1.2 %copy-start = (f32[1024,256]{1,0:T(8,128)S(1)}, f32[1024,256]{1,0:T(8,128)}, u32[]{:S(2)}) copy-start(f32[1024,256]{1,0:T(8,128)} %slab.3) | copy-start | bytes 3145732
  1.9 0.8 %copy-start.2 = (f32[1024,16]{0,1:T(8,128)S(1)}, f32[1024,16]{0,1:T(8,128)}, u32[]{:S(2)}) copy-start(f32[1024,16]{0,1:T(8,128)} %param.4) | copy-start | bytes 196612
  2.7 44.7 %copy-start.1 = (f32[1024,256]{1,0:T(8,128)S(1)}, f32[1024,256]{1,0:T(8,128)}, u32[]{:S(2)}) copy-start(f32[1024,256]{1,0:T(8,128)} %slab.3) | copy-start | bytes 3145732

commit v2 on v1

v2 whole, which is shorter than its diff:
```python
import jax
import jax.numpy as jnp
from jax import lax
from jax.experimental import pallas as pl
from jax.experimental.pallas import tpu as pltpu
from jax.sharding import PartitionSpec as P

MESH = pl.DeviceIdType.MESH
F32 = jnp.float32
BF16 = jnp.bfloat16
NB = 256
ROWS = 1024
COLS = 256
NZ = 16
CHIPS = 16
HALF = 128
WIDTH = 16
LAST = 8
JUMP = 3
REACH = 4


def exchange_kernel(
    pivots, slab, panel, pt, gathered, diag,
    piv, rows, masked, from_sibling, landed, mine, lead_in, piece, piece_in, column,
    local_sem, ring_send, ring_recv, a_send, a_recv, near_send, near_recv, far_send, far_recv, c_send, c_recv,
    lead_send, lead_recv, p_send, p_recv, rs_send, rs_recv, ag_send, ag_recv, sib_send, sib_recv,
):
    p = lax.axis_index("prow")
    z = lax.axis_index("pcol")
    chip = lax.div(p, 2)
    core = lax.rem(p, 2)
    sibling = 2 * chip + 1 - core
    is_root = p == 0
    outer = (core == 1) & (chip > 0)

    def loop(first, last, act):
        def body(o, carry):
            act(o)
            return carry
        lax.fori_loop(first, last, body, 0)

    def near(o):
        return 2 * lax.rem(chip + o, CHIPS) + core

    def above(o):
        return lax.rem(z + o + NZ, NZ)

    barrier = pltpu.get_barrier_semaphore()

    def greet(device):
        pl.semaphore_signal(barrier, inc=1, device_id=device, device_id_type=MESH)

    pivot_copy = pltpu.make_async_copy(pivots, piv, local_sem.at[2])
    panel_copy = pltpu.make_async_copy(panel, pt.at[z], local_sem.at[0])
    slab_copy = pltpu.make_async_copy(slab, rows, local_sem.at[1])
    pivot_copy.start()
    panel_copy.start()
    slab_copy.start()

    for o in range(1, REACH + 1):
        greet((p, above(o)))
        greet((p, above(-o)))
    loop(1, CHIPS, lambda o: greet((near(o), z)))
    greet((sibling, z))

    @pl.when(is_root)
    def _():
        loop(1, CHIPS, lambda o: greet((2 * o + 1, z)))

    @pl.when(outer)
    def _():
        greet((0, z))

    panel_copy.wait()
    for k in range(WIDTH):
        for h in range(2):
            piece[2 * k + h] = pt[z, k : k + 1, h * HALF : (h + 1) * HALF]
    pivot_copy.wait()
    slab_copy.wait()

    row_start = p * ROWS

    def pick(k, carry):
        local = piv[k] - row_start
        held = (local >= 0) & (local < ROWS)
        row = rows[pl.ds(jnp.clip(local, 0, ROWS - 1), 1), :]
        row = jnp.where(held, row, 0.0)
        masked[0, pl.ds(k, 1), :] = row[:, :HALF]
        masked[1, pl.ds(k, 1), :] = row[:, HALF:]
        return carry

    lax.fori_loop(0, NB, pick, 0, unroll=8)

    greeted = 2 * REACH + CHIPS
    pl.semaphore_wait(barrier, greeted + jnp.where(is_root, CHIPS - 1, jnp.where(outer, 1, 0)))

    def remote(src, dst, send, recv, device):
        return pltpu.make_async_remote_copy(
            src_ref=src, dst_ref=dst, send_sem=send, recv_sem=recv, device_id=device, device_id_type=MESH
        )

    def ring_copy(direction, place, half):
        jump = JUMP if place == JUMP else 1
        block = above(-direction * (place - jump))
        part = pt.at[block, pl.ds(8 * half, 8)]
        d = (direction + 1) // 2
        return remote(
            part, part, ring_send.at[d, place, half], ring_recv.at[d, place, half], (p, above(direction * jump))
        )

    def ring_uses(direction, place, half):
        return place < LAST or half == (0 if direction == 1 else 1)

    ring_legs = [(d, h) for h in range(2) for d in (1, -1)]

    def ring_first():
        for place in (JUMP, 1):
            for d, h in ring_legs:
                ring_copy(d, place, h).start()

    def ring_pass(place):
        for d, h in ring_legs:
            if ring_uses(d, place, h):
                ring_copy(d, place, h).wait_recv()
            if place + 1 != JUMP and place < LAST and ring_uses(d, place + 1, h):
                ring_copy(d, place + 1, h).start()

    def a_copy(target):
        return remote(piece.at[target], piece_in.at[z], a_send, a_recv, (target, z))

    def lead_copy(target):
        t_chip, t_core = lax.div(target, 2), lax.rem(target, 2)
        src = rows.at[pl.ds(t_chip * 16, 16), pl.ds(pl.multiple_of(t_core * HALF, HALF), HALF)]
        return remote(src, lead_in, lead_send.at[target], lead_recv, (target, z))

    def rs_copy(o):
        t_chip = lax.rem(chip + o, CHIPS)
        return remote(masked.at[2, pl.ds(t_chip * 16, 16)], landed.at[o], rs_send, rs_recv, (near(o), z))

    def ag_copy(o):
        return remote(mine, gathered.at[core, chip], ag_send, ag_recv, (near(o), z))

    def c_copy(o):
        return remote(column, diag.at[core, chip], c_send, c_recv, (near(o), z))

    def b_copy(source, to, send, recv):
        part = piece_in.at[above(source)]
        return remote(part, part, send, recv, (p, above(to)))

    sib_p = remote(masked.at[1 - core], from_sibling, p_send, p_recv, (sibling, z))
    sib_g = remote(gathered.at[core], gathered.at[core], sib_send.at[0], sib_recv.at[0], (sibling, z))
    sib_d = remote(diag.at[core], diag.at[core], sib_send.at[1], sib_recv.at[1], (sibling, z))
    here = (p, z)
    rs_all = remote(masked.at[2, pl.ds(0, 15 * 16)], landed.at[pl.ds(1, 15)], rs_send, rs_recv, here)
    ag_all = remote(gathered.at[core, pl.ds(0, 15)], gathered.at[core, pl.ds(0, 15)], ag_send, ag_recv, here)
    c_all = remote(diag.at[core, pl.ds(0, 15)], diag.at[core, pl.ds(0, 15)], c_send, c_recv, here)
    near_all = remote(piece_in.at[pl.ds(0, 8)], piece_in.at[pl.ds(0, 8)], near_send, near_recv, here)
    far_all = remote(piece_in.at[pl.ds(0, 7)], piece_in.at[pl.ds(0, 7)], far_send, far_recv, here)
    a_all = remote(piece.at[pl.ds(1, 31)], piece.at[pl.ds(1, 31)], a_send, a_recv, here)

    def a_start():
        @pl.when(is_root)
        def _():
            loop(1, 2 * CHIPS, lambda t: a_copy(t).start())
            piece_in[z] = piece[0]

    def lead_start():
        @pl.when(is_root)
        def _():
            loop(1, 2 * CHIPS, lambda t: lead_copy(t).start())
            lead_in[...] = rows[0:16, 0:HALF]

    def near_start():
        @pl.when(p > 0)
        def _():
            a_copy(p).wait_recv()
        for o in range(1, REACH + 1):
            b_copy(0, o, near_send, near_recv).start()
            b_copy(0, -o, near_send, near_recv).start()

    def far_start():
        near_all.wait_recv()
        for o in range(1, REACH + 1):
            b_copy(-o, REACH, far_send, far_recv).start()
            if o < REACH:
                b_copy(o, -REACH, far_send, far_recv).start()

    def c_start():
        far_all.wait_recv()
        for k in range(NZ):
            column[k : k + 1, :] = piece_in[k]
        diag[core, chip] = column[...]
        loop(1, CHIPS, lambda o: c_copy(o).start())

    def d_start():
        c_all.wait_recv()
        sib_d.start()

    def rs_start():
        sib_p.wait_recv()
        masked[2] = masked[core] + from_sibling[...]
        loop(1, CHIPS, lambda o: rs_copy(o).start())

    def ag_start():
        rs_all.wait_recv()
        @pl.when(p > 0)
        def _():
            lead_copy(p).wait_recv()
        total = masked[2, pl.ds(chip * 16, 16)]
        for o in range(1, CHIPS):
            total = total + landed[o]
        mine[0] = total
        mine[1] = lead_in[...]
        gathered[core, chip] = mine[...]
        loop(1, CHIPS, lambda o: ag_copy(o).start())

    def g_start():
        ag_all.wait_recv()
        sib_g.start()

    a_start()
    sib_p.start()
    ring_first()
    lead_start()
    rs_start()
    ring_pass(1)
    near_start()
    ring_pass(3)
    ag_start()
    far_start()
    ring_pass(4)
    g_start()
    ring_pass(5)
    c_start()
    ring_pass(6)
    d_start()
    ring_pass(7)
    ring_pass(8)
    ring_pass(2)
    sib_g.wait_recv()
    sib_d.wait_recv()

    for copy in (sib_p, sib_g, sib_d, rs_all, ag_all, c_all, near_all, far_all):
        copy.wait_send()
    for place in range(1, LAST + 1):
        for d, h in ring_legs:
            if ring_uses(d, place, h):
                ring_copy(d, place, h).wait_send()

    @pl.when(is_root)
    def _():
        a_all.wait_send()
        loop(1, 2 * CHIPS, lambda t: lead_copy(t).wait_send())


def exchange(slab, panel_t, pivots):
    dma = pltpu.SemaphoreType.DMA
    hbm = pl.BlockSpec(memory_space=pltpu.HBM)
    return pl.pallas_call(
        exchange_kernel,
        name="exchange",
        out_shape=(
            jax.ShapeDtypeStruct((NZ, WIDTH, ROWS), F32),
            jax.ShapeDtypeStruct((2, CHIPS, 2, 16, HALF), F32),
            jax.ShapeDtypeStruct((2, CHIPS, NZ, HALF), F32),
        ),
        in_specs=[hbm] * 3,
        out_specs=(pl.BlockSpec(memory_space=pltpu.VMEM),) * 3,
        scratch_shapes=[
            pltpu.SMEM((NB,), jnp.int32),
            pltpu.VMEM((ROWS, COLS), F32),
            pltpu.VMEM((3, NB, HALF), F32),
            pltpu.VMEM((NB, HALF), F32),
            pltpu.VMEM((CHIPS, 16, HALF), F32),
            pltpu.VMEM((2, 16, HALF), F32),
            pltpu.VMEM((16, HALF), F32),
            pltpu.VMEM((2 * CHIPS, 1, HALF), F32),
            pltpu.VMEM((NZ, 1, HALF), F32),
            pltpu.VMEM((NZ, HALF), F32),
            dma((3,)),
            dma((2, LAST + 1, 2)), dma((2, LAST + 1, 2)),
            dma, dma,
            dma, dma,
            dma, dma,
            dma, dma,
            dma((2 * CHIPS,)), dma,
            dma, dma,
            dma, dma,
            dma, dma,
            dma((2,)), dma((2,)),
        ],
        compiler_params=pltpu.CompilerParams(
            collective_id=0, has_side_effects=True, vmem_limit_bytes=24 * 1024 * 1024
        ),
    )(pivots, slab, panel_t)


def split(a):
    high = a.astype(BF16)
    return high, (a - high.astype(F32)).astype(BF16)


def dot3(a, b, dims=(((1,), (0,)), ((), ()))):
    def one(x, y):
        return lax.dot_general(x, y, dims, preferred_element_type=F32)

    return one(a[0], b[0]) + (one(a[0], b[1]) + one(a[1], b[0]))


def invert(lower):
    row = lax.broadcasted_iota(jnp.int32, (NB, NB), 0)
    col = lax.broadcasted_iota(jnp.int32, (NB, NB), 1)
    base = 16
    blocks = NB // base
    on_diag = (row // base) == (col // base)
    packed = jnp.sum(jnp.where(on_diag, lower, 0.0).reshape(blocks, base, NB), axis=0)
    small_row = lax.broadcasted_iota(jnp.int32, (base, NB), 0)
    small_col = lax.broadcasted_iota(jnp.int32, (base, NB), 1)
    lane = lax.broadcasted_iota(jnp.int32, (base, HALF), 1)
    inverse = jnp.where(small_row == small_col % base, 1.0, 0.0)
    for k in range(base - 1):
        index = (lane // base) * base + k
        factor = jnp.concatenate(
            [jnp.take_along_axis(packed[:, h * HALF : (h + 1) * HALF], index, axis=1) for h in range(2)], axis=1
        )
        inverse = inverse - factor * inverse[k : k + 1, :]
    inverse = jnp.where(on_diag, jnp.concatenate([inverse] * blocks, axis=0), 0.0)
    size = base
    while size < NB:
        same = (row // (2 * size)) == (col // (2 * size))
        below = same & ((row // size) % 2 == 1) & ((col // size) % 2 == 0)
        corner = jnp.where(below, lower, 0.0)
        parts = split(inverse)
        inverse = inverse - dot3(parts, split(dot3(split(corner), parts)))
        size *= 2
    return inverse


def update_kernel(piv, slab, pt, gathered, diag, out, rows, leading, upper_t, result, load_sem, store_sem):
    p = lax.axis_index("prow")
    load = pltpu.make_async_copy(slab, rows.at[pl.ds(0, ROWS)], load_sem)
    load.start()

    for h in range(2):
        for z in range(NZ):
            upper_t[z * 16 : (z + 1) * 16, h * HALF : (h + 1) * HALF] = diag[h, pl.ds(z, 16, stride=NZ), :]
    row = lax.broadcasted_iota(jnp.int32, (NB, NB), 0)
    col = lax.broadcasted_iota(jnp.int32, (NB, NB), 1)
    lower = jnp.where(row > col, upper_t[...].T, 0.0)
    inverse = invert(lower)
    pivot_rows = jnp.concatenate([gathered[h, :, 0].reshape(NB, HALF) for h in range(2)], axis=1)
    upper = dot3(split(inverse), split(pivot_rows))
    upper_parts = split(upper)

    load.wait()

    def swap(k, carry):
        local = piv[k] - p * ROWS
        held = (local >= 0) & (local < ROWS)
        target = jnp.where(held, local, ROWS)
        rows[pl.ds(target, 1), :] = leading[pl.ds(k, 1), :]
        return carry

    for h in range(2):
        leading[:, h * HALF : (h + 1) * HALF] = gathered[h, :, 1].reshape(NB, HALF)
    lax.fori_loop(0, NB, swap, 0, unroll=8)

    chunk = 256
    for n in range(ROWS // chunk):
        block = pt[:, n * chunk : (n + 1) * chunk]
        product = dot3(split(block), upper_parts, (((0,), (0,)), ((), ())))
        value = rows[n * chunk : (n + 1) * chunk, :] - product
        if n == 0:
            value = jnp.where(p == 0, upper, value)
        result[n * chunk : (n + 1) * chunk, :] = value
        pltpu.make_async_copy(
            result.at[pl.ds(n * chunk, chunk)], out.at[pl.ds(n * chunk, chunk)], store_sem.at[n]
        ).start()
    for n in range(ROWS // chunk):
        pltpu.make_async_copy(
            result.at[pl.ds(n * chunk, chunk)], out.at[pl.ds(n * chunk, chunk)], store_sem.at[n]
        ).wait()


def finish(slab, pivots, pt, gathered, diag):
    vmem = pl.BlockSpec(memory_space=pltpu.VMEM)
    hbm = pl.BlockSpec(memory_space=pl.ANY)
    return pl.pallas_call(
        update_kernel,
        name="finish",
        out_shape=jax.ShapeDtypeStruct((ROWS, COLS), F32),
        in_specs=[pl.BlockSpec(memory_space=pltpu.SMEM), hbm, vmem, vmem, vmem],
        out_specs=hbm,
        scratch_shapes=[
            pltpu.VMEM((ROWS + 8, COLS), F32),
            pltpu.VMEM((NB, COLS), F32),
            pltpu.VMEM((NB, NB), F32),
            pltpu.VMEM((ROWS, COLS), F32),
            pltpu.SemaphoreType.DMA,
            pltpu.SemaphoreType.DMA((4,)),
        ],
        compiler_params=pltpu.CompilerParams(vmem_limit_bytes=32 * 1024 * 1024),
    )(pivots, slab, pt.reshape(NZ * WIDTH, ROWS), gathered, diag.reshape(2, NB, HALF))


def local(slab, panel, pivots):
    pt, gathered, diag = exchange(slab, panel.T, pivots)
    return finish(slab, pivots, pt, gathered, diag)


def solution(mesh):
    return jax.shard_map(
        local,
        mesh=mesh,
        in_specs=(P("prow", "pcol"), P("prow", "pcol"), P()),
        out_specs=P("prow", "pcol"),
        check_vma=False,
    )
```

time: 54.2 us -> 51.4 us (0.948)
  the two profiles are of different devices: /device:TPU:18 before, /device:TPU:32 now
where the time goes in v2:
time: 51.4 us; the launch traced here: 51.2 us
  Pallas kernels  48.4 us (94%)
  local copies, waits for them, and re-layouts  2.75 us (5%)
    pallas_call x1, Pallas kernels, exchange(): pl.pallas_call(exchange_kernel, name='exchange', out_shape=(jax.ShapeDtyp...  41.9 us
    pallas_call x1, Pallas kernels, finish(): pl.pallas_call(update_kernel, name='finish', out_shape=jax.ShapeDtypeStru...  6.53 us
    unnamed x8, local copies, waits for them, and re-layouts  2.75 us

profile of v2, /device:TPU:32, one launch (start us, length us, event | category | flops | bytes accessed | tf_op | source)
XLA Modules:
  0.0 51.2 jit_solution(13911319397463993187)
XLA Ops:
  0.0 0.0 copy-start.3
  0.0 0.7 %copy-done.3 = s32[256]{0:T(256)S(1)} copy-done((s32[256]{0:T(256)S(1)}, s32[256]{0:T(256)}, u32[]{:S(2)}) %copy-start.3) | copy-done | bytes 1048
  0.7 0.0 copy-start
  0.7 1.2 %copy-done = f32[1024,256]{1,0:T(8,128)S(1)} copy-done((f32[1024,256]{1,0:T(8,128)S(1)}, f32[1024,256]{1,0:T(8,128)}, u32[]{:S(2)}) %copy-start) | copy-done | bytes 1048600
  1.9 0.0 copy-start.2
  1.9 0.8 %copy-done.2 = f32[1024,16]{0,1:T(8,128)S(1)} copy-done((f32[1024,16]{0,1:T(8,128)S(1)}, f32[1024,16]{0,1:T(8,128)}, u32[]{:S(2)}) %copy-start.2) | copy-done | bytes 65560
  2.7 0.0 copy-start.1
  2.7 41.9 %exchange.1 = (f32[16,16,1024]{2,1,0:T(8,128)S(1)}, f32[2,16,2,16,128]{4,3,2,1,0:T(8,128)S(1)}, f32[2,16,16,128]{3,2,1,0:T(8,128)S(1)}) custom-call(s32[256]{0:T(256)S(1)} %copy-done.3, f32[1024,256]{1,0:T(8,128)S(1)} %copy-done, f32[16,1024]{1,0:T(8,128)S(1)} %bitcast.5), custom_call_target="tpu_custom_call" | custom-call | tf_op jit(solution)/shard_map/exchange/pallas_call | solution.py:260
  44.6 0.0 copy-done.1
  44.6 6.5 %finish.1 = f32[1024,256]{1,0:T(8,128)} custom-call(s32[256]{0:T(256)S(1)} %copy-done.3, f32[1024,256]{1,0:T(8,128)S(1)} %copy-done.1, f32[256,1024]{1,0:T(8,128)S(1)} %bitcast.3, f32[2,16,2,16,128]{4,3,2,1,0:T(8,128)S(1)} %get-tuple-element.9.gathered, f32[2,256,128]{2,1,0:T(8,128)S(1)} %bitcast.4), custom_call_target="tpu_custom_call" | custom-call | tf_op jit(solution)/shard_map/finish/pallas_call | solution.py:389
Async XLA Ops:
  0.0 0.7 %copy-start.3 = (s32[256]{0:T(256)S(1)}, s32[256]{0:T(256)}, u32[]{:S(2)}) copy-start(s32[256]{0:T(256)} %piv.1) | copy-start | bytes 3076
  0.7 1.2 %copy-start = (f32[1024,256]{1,0:T(8,128)S(1)}, f32[1024,256]{1,0:T(8,128)}, u32[]{:S(2)}) copy-start(f32[1024,256]{1,0:T(8,128)} %slab.3) | copy-start | bytes 3145732
  1.9 0.8 %copy-start.2 = (f32[1024,16]{0,1:T(8,128)S(1)}, f32[1024,16]{0,1:T(8,128)}, u32[]{:S(2)}) copy-start(f32[1024,16]{0,1:T(8,128)} %param.4) | copy-start | bytes 196612
  2.7 41.9 %copy-start.1 = (f32[1024,256]{1,0:T(8,128)S(1)}, f32[1024,256]{1,0:T(8,128)}, u32[]{:S(2)}) copy-start(f32[1024,256]{1,0:T(8,128)} %slab.3) | copy-start | bytes 3145732

commit v3 on v2

v3 whole, which is shorter than its diff:
```python
import jax
import jax.numpy as jnp
from jax import lax
from jax.experimental import pallas as pl
from jax.experimental.pallas import tpu as pltpu
from jax.sharding import PartitionSpec as P

MESH = pl.DeviceIdType.MESH
F32 = jnp.float32
BF16 = jnp.bfloat16
NB = 256
ROWS = 1024
COLS = 256
NZ = 16
CHIPS = 16
HALF = 128
WIDTH = 16
LAST = 8
REACH = 4
CHUNK = 256
BASE = 32


def exchange_kernel(
    pivots, pivot_row, slab, panel, out,
    pt, gathered, wide, piv, pivot_lanes, upper_t, leading, panel_high, panel_low, rows, masked, from_sibling, landed, mine, lead_in, piece, piece_in, column,
    local_sem, ring_send, ring_recv, a_send, a_recv, near_send, near_recv, far_send, far_recv, c_send, c_recv,
    lead_send, lead_recv, p_send, p_recv, rs_send, rs_recv, ag_send, ag_recv, sib_send, sib_recv, store_sem,
):
    p = lax.axis_index("prow")
    z = lax.axis_index("pcol")
    chip = lax.div(p, 2)
    core = lax.rem(p, 2)
    sibling = 2 * chip + 1 - core
    is_root = p == 0
    outer = (core == 1) & (chip > 0)

    def loop(first, last, act):
        def body(o, carry):
            act(o)
            return carry
        lax.fori_loop(first, last, body, 0)

    def near(o):
        return 2 * lax.rem(chip + o, CHIPS) + core

    def above(o):
        return lax.rem(z + o + NZ, NZ)

    barrier = pltpu.get_barrier_semaphore()

    def greet(device):
        pl.semaphore_signal(barrier, inc=1, device_id=device, device_id_type=MESH)

    pivot_copy = pltpu.make_async_copy(pivots, piv, local_sem.at[2])
    panel_copy = pltpu.make_async_copy(panel, pt.at[z], local_sem.at[0])
    slab_copy = pltpu.make_async_copy(slab, rows, local_sem.at[1])
    lanes_copy = pltpu.make_async_copy(pivot_row, pivot_lanes, local_sem.at[3])
    pivot_copy.start()
    lanes_copy.start()
    panel_copy.start()
    slab_copy.start()

    for o in range(1, REACH + 1):
        greet((p, above(o)))
        greet((p, above(-o)))
    loop(1, CHIPS, lambda o: greet((near(o), z)))
    greet((sibling, z))

    @pl.when(is_root)
    def _():
        loop(1, CHIPS, lambda o: greet((2 * o + 1, z)))

    @pl.when(outer)
    def _():
        greet((0, z))

    panel_copy.wait()
    for k in range(WIDTH):
        for h in range(2):
            piece[2 * k + h] = pt[z, k : k + 1, h * HALF : (h + 1) * HALF]
    pivot_copy.wait()
    lanes_copy.wait()
    slab_copy.wait()

    row_start = p * ROWS

    def pick(k, carry):
        local = piv[k] - row_start
        held = (local >= 0) & (local < ROWS)
        row = rows[pl.ds(jnp.clip(local, 0, ROWS - 1), 1), :]
        row = jnp.where(held, row, 0.0)
        masked[0, pl.ds(k, 1), :] = row[:, :HALF]
        masked[1, pl.ds(k, 1), :] = row[:, HALF:]
        return carry

    lax.fori_loop(0, NB, pick, 0, unroll=8)

    greeted = 2 * REACH + CHIPS
    pl.semaphore_wait(barrier, greeted + jnp.where(is_root, CHIPS - 1, jnp.where(outer, 1, 0)))

    def remote(src, dst, send, recv, device):
        return pltpu.make_async_remote_copy(
            src_ref=src, dst_ref=dst, send_sem=send, recv_sem=recv, device_id=device, device_id_type=MESH
        )

    def ring_copy(direction, place, half):
        jump = 2 - place % 2
        part = pt.at[above(-direction * (place - jump)), pl.ds(8 * half, 8)]
        d = (direction + 1) // 2
        return remote(
            part, part, ring_send.at[d, place, half], ring_recv.at[d, place, half], (p, above(direction * jump))
        )

    def ring_uses(direction, place, half):
        return place < LAST or (place == LAST and half == (0 if direction == 1 else 1))

    ring_legs = [(d, h) for h in range(2) for d in (1, -1)]

    def ring_pass(place):
        for d, h in ring_legs:
            if place > 0 and ring_uses(d, place, h):
                ring_copy(d, place, h).wait_recv()
            if place % 2 == 0:
                for later in (place + 2, place + 1):
                    if ring_uses(d, later, h):
                        ring_copy(d, later, h).start()

    def a_copy(target):
        return remote(piece.at[target], piece_in.at[z], a_send, a_recv, (target, z))

    def lead_copy(target):
        t_chip, t_core = lax.div(target, 2), lax.rem(target, 2)
        src = rows.at[pl.ds(t_chip * 16, 16), pl.ds(pl.multiple_of(t_core * HALF, HALF), HALF)]
        return remote(src, lead_in, lead_send, lead_recv, (target, z))

    def rs_copy(o):
        t_chip = lax.rem(chip + o, CHIPS)
        return remote(masked.at[2, pl.ds(t_chip * 16, 16)], landed.at[o], rs_send, rs_recv, (near(o), z))

    def ag_copy(o):
        return remote(mine, gathered.at[core, chip], ag_send, ag_recv, (near(o), z))

    def c_copy(o):
        return remote(column, wide.at[core, pl.ds(pl.multiple_of(16 * chip, 16), 16)], c_send, c_recv, (near(o), z))

    def b_copy(source, to, send, recv):
        part = piece_in.at[above(source)]
        return remote(part, part, send, recv, (p, above(to)))

    sib_p = remote(masked.at[1 - core], from_sibling, p_send, p_recv, (sibling, z))
    sib_g = remote(gathered.at[core], gathered.at[core], sib_send.at[0], sib_recv.at[0], (sibling, z))
    sib_d = remote(wide.at[core], wide.at[core], sib_send.at[1], sib_recv.at[1], (sibling, z))
    here = (p, z)
    rs_all = remote(masked.at[2, pl.ds(0, 15 * 16)], landed.at[pl.ds(1, 15)], rs_send, rs_recv, here)
    ag_all = remote(gathered.at[core, pl.ds(0, 15)], gathered.at[core, pl.ds(0, 15)], ag_send, ag_recv, here)
    c_all = remote(wide.at[core, pl.ds(0, 240)], wide.at[core, pl.ds(0, 240)], c_send, c_recv, here)
    near_all = remote(piece_in.at[pl.ds(0, 8)], piece_in.at[pl.ds(0, 8)], near_send, near_recv, here)
    far_all = remote(piece_in.at[pl.ds(0, 7)], piece_in.at[pl.ds(0, 7)], far_send, far_recv, here)
    lead_all = remote(rows.at[pl.ds(0, 31 * 8)], rows.at[pl.ds(0, 31 * 8)], lead_send, lead_recv, here)
    a_all = remote(piece.at[pl.ds(1, 31)], piece.at[pl.ds(1, 31)], a_send, a_recv, here)

    def a_start():
        @pl.when(is_root)
        def _():
            loop(1, 2 * CHIPS, lambda t: a_copy(t).start())
            piece_in[z] = piece[0]

    def lead_start():
        @pl.when(is_root)
        def _():
            loop(1, 2 * CHIPS, lambda t: lead_copy(t).start())
            lead_in[...] = rows[0:16, 0:HALF]

    def near_start():
        @pl.when(p > 0)
        def _():
            a_copy(p).wait_recv()
        for o in range(1, REACH + 1):
            b_copy(0, o, near_send, near_recv).start()
            b_copy(0, -o, near_send, near_recv).start()

    def far_start():
        near_all.wait_recv()
        for o in range(1, REACH + 1):
            b_copy(-o, REACH, far_send, far_recv).start()
            if o < REACH:
                b_copy(o, -REACH, far_send, far_recv).start()

    def c_start():
        far_all.wait_recv()
        for k in range(NZ):
            column[k : k + 1, :] = piece_in[k]
        wide[core, pl.ds(pl.multiple_of(16 * chip, 16), 16)] = column[...]
        loop(1, CHIPS, lambda o: c_copy(o).start())

    def d_start():
        c_all.wait_recv()
        sib_d.start()

    def rs_start():
        sib_p.wait_recv()
        masked[2] = masked[core] + from_sibling[...]
        loop(1, CHIPS, lambda o: rs_copy(o).start())

    def ag_start():
        rs_all.wait_recv()
        @pl.when(p > 0)
        def _():
            lead_copy(p).wait_recv()
        total = masked[2, pl.ds(chip * 16, 16)]
        for o in range(1, CHIPS):
            total = total + landed[o]
        mine[0] = total
        mine[1] = lead_in[...]
        gathered[core, chip] = mine[...]
        loop(1, CHIPS, lambda o: ag_copy(o).start())

    def g_start():
        ag_all.wait_recv()
        sib_g.start()

    def swap_rows():
        sib_g.wait_recv()
        for h in range(2):
            leading[:, h * HALF : (h + 1) * HALF] = gathered[h, :, 1].reshape(NB, HALF)
        lead_high, lead_low = split(leading[...])
        ones = jnp.ones((NB, COLS), BF16)
        for n in range(ROWS // CHUNK):
            index = lax.broadcasted_iota(jnp.int32, (CHUNK, NB), 0) + (row_start + n * CHUNK)
            chosen = jnp.where(index == pivot_lanes[...], 1.0, 0.0).astype(BF16)
            replaced = dot1(chosen, lead_high) + dot1(chosen, lead_low)
            part = slice(n * CHUNK, (n + 1) * CHUNK)
            rows[part, :] = jnp.where(dot1(chosen, ones) > 0.5, replaced, rows[part, :])

    def split_panel():
        for n in range(ROWS // CHUNK):
            part = slice(n * CHUNK, (n + 1) * CHUNK)
            high, low = split(pt[:, :, part].reshape(NB, CHUNK).T)
            panel_high[part, :] = high
            panel_low[part, :] = low

    a_start()
    sib_p.start()
    ring_pass(0)
    lead_start()
    rs_start()
    near_start()
    ring_pass(2)
    ag_start()
    far_start()
    ring_pass(4)
    ring_pass(1)
    c_start()
    ring_pass(6)
    g_start()
    ring_pass(3)
    @pl.when(is_root)
    def _():
        lead_all.wait_send()
    d_start()
    swap_rows()
    for place in (5, 7, 8):
        ring_pass(place)
    split_panel()
    sib_d.wait_recv()

    for h in range(2):
        for k in range(NZ):
            upper_t[k * 16 : (k + 1) * 16, h * HALF : (h + 1) * HALF] = wide[h, pl.ds(k, 16, stride=NZ), :]
    first, second = slice(0, HALF), slice(HALF, NB)
    corner = split(upper_t[first, second].T)
    top = split(invert(upper_t[first, first].T))
    bottom = split(invert(upper_t[second, second].T))

    def pivot_half(h):
        return jnp.concatenate([gathered[c, 8 * h : 8 * h + 8, 0].reshape(HALF, HALF) for c in range(2)], axis=1)

    upper_first = dot3(top, split(pivot_half(0)))
    upper_second = dot3(bottom, split(pivot_half(1) - dot3(corner, split(upper_first))))
    upper = jnp.concatenate([upper_first, upper_second], axis=0)
    upper_parts = split(upper)

    def store(n):
        part = pl.ds(n * CHUNK, CHUNK)
        return pltpu.make_async_copy(rows.at[part], out.at[part], store_sem.at[n])

    for n in range(ROWS // CHUNK):
        part = slice(n * CHUNK, (n + 1) * CHUNK)
        value = rows[part, :] - dot3((panel_high[part, :], panel_low[part, :]), upper_parts)
        if n == 0:
            value = jnp.where(is_root, upper, value)
        rows[part, :] = value
        store(n).start()

    for copy in (sib_p, sib_g, sib_d, rs_all, ag_all, c_all, near_all, far_all):
        copy.wait_send()
    for place in range(1, LAST + 1):
        for d, h in ring_legs:
            if ring_uses(d, place, h):
                ring_copy(d, place, h).wait_send()

    @pl.when(is_root)
    def _():
        a_all.wait_send()

    for n in range(ROWS // CHUNK):
        store(n).wait()


def split(a):
    high = a.astype(BF16)
    return high, (a - high.astype(F32)).astype(BF16)


def dot1(a, b):
    return jnp.dot(a, b, preferred_element_type=F32)


def dot3(a, b):
    return dot1(a[0], b[0]) + (dot1(a[0], b[1]) + dot1(a[1], b[0]))


def invert(square):
    row = lax.broadcasted_iota(jnp.int32, (HALF, HALF), 0)
    col = lax.broadcasted_iota(jnp.int32, (HALF, HALF), 1)
    lower = jnp.where(row > col, square, 0.0)
    blocks = HALF // BASE
    on_diag = (row // BASE) == (col // BASE)
    packed = jnp.sum(jnp.where(on_diag, lower, 0.0).reshape(blocks, BASE, HALF), axis=0)
    small_row = lax.broadcasted_iota(jnp.int32, (BASE, HALF), 0)
    small_col = lax.broadcasted_iota(jnp.int32, (BASE, HALF), 1)
    inverse = jnp.where(small_row == small_col % BASE, 1.0, 0.0)
    for k in range(BASE - 1):
        factor = jnp.take_along_axis(packed, (small_col // BASE) * BASE + k, axis=1)
        inverse = inverse - factor * inverse[k : k + 1, :]
    inverse = jnp.where(on_diag, jnp.concatenate([inverse] * blocks, axis=0), 0.0)
    size = BASE
    while size < HALF:
        same = (row // (2 * size)) == (col // (2 * size))
        below = same & ((row // size) % 2 == 1) & ((col // size) % 2 == 0)
        parts = split(inverse)
        inverse = inverse - dot3(parts, split(dot3(split(jnp.where(below, lower, 0.0)), parts)))
        size *= 2
    return inverse


def local(slab, panel, pivots):
    dma = pltpu.SemaphoreType.DMA
    hbm = pl.BlockSpec(memory_space=pltpu.HBM)
    return pl.pallas_call(
        exchange_kernel,
        name="exchange",
        out_shape=jax.ShapeDtypeStruct((ROWS, COLS), F32),
        in_specs=[hbm] * 4,
        out_specs=hbm,
        scratch_shapes=[
            pltpu.VMEM((NZ, WIDTH, ROWS), F32),
            pltpu.VMEM((2, CHIPS, 2, 16, HALF), F32),
            pltpu.VMEM((2, NB, HALF), F32),
            pltpu.SMEM((NB,), jnp.int32),
            pltpu.VMEM((1, NB), jnp.int32),
            pltpu.VMEM((NB, NB), F32),
            pltpu.VMEM((NB, COLS), F32),
            pltpu.VMEM((ROWS, NB), BF16),
            pltpu.VMEM((ROWS, NB), BF16),
            pltpu.VMEM((ROWS, COLS), F32),
            pltpu.VMEM((3, NB, HALF), F32),
            pltpu.VMEM((NB, HALF), F32),
            pltpu.VMEM((CHIPS, 16, HALF), F32),
            pltpu.VMEM((2, 16, HALF), F32),
            pltpu.VMEM((16, HALF), F32),
            pltpu.VMEM((2 * CHIPS, 1, HALF), F32),
            pltpu.VMEM((NZ, 1, HALF), F32),
            pltpu.VMEM((NZ, HALF), F32),
            dma((4,)),
            dma((2, LAST + 1, 2)), dma((2, LAST + 1, 2)),
            dma, dma,
            dma, dma,
            dma, dma,
            dma, dma,
            dma, dma,
            dma, dma,
            dma, dma,
            dma, dma,
            dma((2,)), dma((2,)),
            dma((ROWS // CHUNK,)),
        ],
        compiler_params=pltpu.CompilerParams(
            collective_id=0, has_side_effects=True, vmem_limit_bytes=63 * 1000 * 1024
        ),
    )(pivots, pivots.reshape(1, NB), slab, panel.T)


def solution(mesh):
    return jax.shard_map(
        local,
        mesh=mesh,
        in_specs=(P("prow", "pcol"), P("prow", "pcol"), P()),
        out_specs=P("prow", "pcol"),
        check_vma=False,
    )
```

time: 51.4 us -> 43.1 us (0.84)
  the two profiles are of different devices: /device:TPU:32 before, /device:TPU:1 now
where the time goes in v3:
time: 43.1 us; the launch traced here: 42.9 us
  Pallas kernels  40.7 us (94%)
  local copies, waits for them, and re-layouts  2.26 us (5%)
    pallas_call x1, Pallas kernels, local(): pl.pallas_call(exchange_kernel, name='exchange', out_shape=jax.ShapeDtype...  40.7 us
    unnamed x1, local copies, waits for them, and re-layouts  2.26 us

profile of v3, /device:TPU:1, one launch (start us, length us, event | category | flops | bytes accessed | tf_op | source)
XLA Modules:
  0.0 42.9 jit_solution(12620075655312795113)
XLA Ops:
  0.0 40.7 %exchange.1 = f32[1024,256]{1,0:T(8,128)} custom-call(s32[256]{0:T(256)} %pivots.1, s32[1,256]{1,0:T(1,128)} %bitcast.3, f32[1024,256]{1,0:T(8,128)} %slab.1, f32[16,1024]{1,0:T(8,128)} %bitcast.2), custom_call_target="tpu_custom_call" | custom-call | tf_op jit(solution)/shard_map/exchange/pallas_call | solution.py:351
  40.7 2.3 %copy.5 = f32[1024,256]{1,0:T(8,128)} copy(f32[1024,256]{1,0:T(8,128)} %exchange.1) | data formatting | bytes 2097152

commit v4 on v3

--- a/solution.py
+++ b/solution.py
@@ -24,8 +24,8 @@
 def exchange_kernel(
     pivots, pivot_row, slab, panel, out,
     pt, gathered, wide, piv, pivot_lanes, upper_t, leading, panel_high, panel_low, rows, masked, from_sibling, landed, mine, lead_in, piece, piece_in, column,
-    local_sem, ring_send, ring_recv, a_send, a_recv, near_send, near_recv, far_send, far_recv, c_send, c_recv,
-    lead_send, lead_recv, p_send, p_recv, rs_send, rs_recv, ag_send, ag_recv, sib_send, sib_recv, store_sem,
+    local_sem, ring_send, ring_recv, a_send, a_recv, b_send, b_recv, c_send, c_recv,
+    lead_send, lead_recv, p_send, p_recv, rs_send, rs_recv, ag_send, ag_recv, g_send, g_recv, store_sem, known,
 ):
     p = lax.axis_index("prow")
     z = lax.axis_index("pcol")
@@ -47,6 +47,19 @@
     def above(o):
         return lax.rem(z + o + NZ, NZ)
 
+    x, y = lax.div(chip, 4), lax.rem(chip, 4)
+    x_odd, y_odd = lax.rem(x, 2), lax.rem(y, 2)
+    across, along = 4 - 8 * x_odd, 1 - 2 * y_odd
+    square = [(chip + move, c) for move in (across + along, across, along) for c in (core, 1 - core)]
+    square.append((chip, 1 - core))
+
+    def part_of(target):
+        target_chip = lax.div(target, 2)
+        return 4 * lax.rem(lax.div(target_chip, 4), 2) + 2 * lax.rem(target_chip, 2) + lax.rem(target, 2)
+
+    mine_part = lax.div(part_of(p), 2)
+    relay = pl.ds(pl.multiple_of(core * NB + 64 * mine_part, 64), 64)
+
     barrier = pltpu.get_barrier_semaphore()
 
     def greet(device):
@@ -65,6 +78,8 @@
         greet((p, above(o)))
         greet((p, above(-o)))
     loop(1, CHIPS, lambda o: greet((near(o), z)))
+    for other, c in square[1::2]:
+        greet((2 * other + c, z))
     greet((sibling, z))
 
     @pl.when(is_root)
@@ -78,7 +93,7 @@
     panel_copy.wait()
     for k in range(WIDTH):
         for h in range(2):
-            piece[2 * k + h] = pt[z, k : k + 1, h * HALF : (h + 1) * HALF]
+            piece[2 * (k % 4) + h, k // 4 : k // 4 + 1, :] = pt[z, k : k + 1, h * HALF : (h + 1) * HALF]
     pivot_copy.wait()
     lanes_copy.wait()
     slab_copy.wait()
@@ -96,8 +111,11 @@
 
     lax.fori_loop(0, NB, pick, 0, unroll=8)
 
-    greeted = 2 * REACH + CHIPS
+    greeted = 2 * REACH + CHIPS + 3
     pl.semaphore_wait(barrier, greeted + jnp.where(is_root, CHIPS - 1, jnp.where(outer, 1, 0)))
+
+    for o in (REACH, -REACH):
+        pl.semaphore_signal(known, inc=1, device_id=(p, above(o)), device_id_type=MESH)
 
     def remote(src, dst, send, recv, device):
         return pltpu.make_async_remote_copy(
@@ -127,7 +145,7 @@
                         ring_copy(d, later, h).start()
 
     def a_copy(target):
-        return remote(piece.at[target], piece_in.at[z], a_send, a_recv, (target, z))
+        return remote(piece.at[part_of(target)], piece_in.at[z], a_send, a_recv, (target, z))
 
     def lead_copy(target):
         t_chip, t_core = lax.div(target, 2), lax.rem(target, 2)
@@ -141,24 +159,19 @@
     def ag_copy(o):
         return remote(mine, gathered.at[core, chip], ag_send, ag_recv, (near(o), z))
 
-    def c_copy(o):
-        return remote(column, wide.at[core, pl.ds(pl.multiple_of(16 * chip, 16), 16)], c_send, c_recv, (near(o), z))
-
-    def b_copy(source, to, send, recv):
-        part = piece_in.at[above(source)]
-        return remote(part, part, send, recv, (p, above(to)))
+    def b_copy(o):
+        return remote(piece_in.at[z], piece_in.at[z], b_send, b_recv, (p, above(o)))
 
     sib_p = remote(masked.at[1 - core], from_sibling, p_send, p_recv, (sibling, z))
-    sib_g = remote(gathered.at[core], gathered.at[core], sib_send.at[0], sib_recv.at[0], (sibling, z))
-    sib_d = remote(wide.at[core], wide.at[core], sib_send.at[1], sib_recv.at[1], (sibling, z))
+    sib_g = remote(gathered.at[core], gathered.at[core], g_send, g_recv, (sibling, z))
+    c_copies = [remote(wide.at[relay], wide.at[relay], c_send, c_recv, (2 * other + c, z)) for other, c in square]
     here = (p, z)
     rs_all = remote(masked.at[2, pl.ds(0, 15 * 16)], landed.at[pl.ds(1, 15)], rs_send, rs_recv, here)
     ag_all = remote(gathered.at[core, pl.ds(0, 15)], gathered.at[core, pl.ds(0, 15)], ag_send, ag_recv, here)
-    c_all = remote(wide.at[core, pl.ds(0, 240)], wide.at[core, pl.ds(0, 240)], c_send, c_recv, here)
-    near_all = remote(piece_in.at[pl.ds(0, 8)], piece_in.at[pl.ds(0, 8)], near_send, near_recv, here)
-    far_all = remote(piece_in.at[pl.ds(0, 7)], piece_in.at[pl.ds(0, 7)], far_send, far_recv, here)
+    c_all = remote(wide.at[pl.ds(0, 448)], wide.at[pl.ds(0, 448)], c_send, c_recv, here)
+    b_all = remote(piece_in.at[pl.ds(0, 15)], piece_in.at[pl.ds(0, 15)], b_send, b_recv, here)
     lead_all = remote(rows.at[pl.ds(0, 31 * 8)], rows.at[pl.ds(0, 31 * 8)], lead_send, lead_recv, here)
-    a_all = remote(piece.at[pl.ds(1, 31)], piece.at[pl.ds(1, 31)], a_send, a_recv, here)
+    a_all = remote(masked.at[0, pl.ds(0, 124)], masked.at[0, pl.ds(0, 124)], a_send, a_recv, here)
 
     def a_start():
         @pl.when(is_root)
@@ -172,31 +185,21 @@
             loop(1, 2 * CHIPS, lambda t: lead_copy(t).start())
             lead_in[...] = rows[0:16, 0:HALF]
 
-    def near_start():
+    def b_start():
         @pl.when(p > 0)
         def _():
             a_copy(p).wait_recv()
-        for o in range(1, REACH + 1):
-            b_copy(0, o, near_send, near_recv).start()
-            b_copy(0, -o, near_send, near_recv).start()
-
-    def far_start():
-        near_all.wait_recv()
-        for o in range(1, REACH + 1):
-            b_copy(-o, REACH, far_send, far_recv).start()
-            if o < REACH:
-                b_copy(o, -REACH, far_send, far_recv).start()
+        pl.semaphore_wait(known, 2)
+        for o in (8, 7, 9, 6, 10, 5, 11, 4, 12, 3, 13, 2, 14, 1, 15):
+            b_copy(o).start()
 
     def c_start():
-        far_all.wait_recv()
+        b_all.wait_recv()
         for k in range(NZ):
-            column[k : k + 1, :] = piece_in[k]
-        wide[core, pl.ds(pl.multiple_of(16 * chip, 16), 16)] = column[...]
-        loop(1, CHIPS, lambda o: c_copy(o).start())
-
-    def d_start():
-        c_all.wait_recv()
-        sib_d.start()
+            column[4 * k : 4 * k + 4, :] = piece_in[k]
+        wide[relay, :] = column[...]
+        for copy in c_copies:
+            copy.start()
 
     def rs_start():
         sib_p.wait_recv()
@@ -233,10 +236,11 @@
             part = slice(n * CHUNK, (n + 1) * CHUNK)
             rows[part, :] = jnp.where(dot1(chosen, ones) > 0.5, replaced, rows[part, :])
 
-    def split_panel():
-        for n in range(ROWS // CHUNK):
-            part = slice(n * CHUNK, (n + 1) * CHUNK)
-            high, low = split(pt[:, :, part].reshape(NB, CHUNK).T)
+    def split_blocks(*places):
+        for place in places:
+            block = above(place)
+            high, low = split(pt[block])
+            part = pl.ds(pl.multiple_of(WIDTH * block, WIDTH), WIDTH)
             panel_high[part, :] = high
             panel_low[part, :] = low
 
@@ -245,33 +249,30 @@
     ring_pass(0)
     lead_start()
     rs_start()
-    near_start()
+    b_start()
     ring_pass(2)
+    split_blocks(0, 2, -2)
     ag_start()
-    far_start()
     ring_pass(4)
     ring_pass(1)
+    split_blocks(4, -4, 1, -1)
     c_start()
     ring_pass(6)
     g_start()
     ring_pass(3)
+    split_blocks(3, -3, 6, -6)
     @pl.when(is_root)
     def _():
         lead_all.wait_send()
-    d_start()
     swap_rows()
-    for place in (5, 7, 8):
-        ring_pass(place)
-    split_panel()
-    sib_d.wait_recv()
+    c_all.wait_recv()
 
     for h in range(2):
-        for k in range(NZ):
-            upper_t[k * 16 : (k + 1) * 16, h * HALF : (h + 1) * HALF] = wide[h, pl.ds(k, 16, stride=NZ), :]
-    first, second = slice(0, HALF), slice(HALF, NB)
-    corner = split(upper_t[first, second].T)
-    top = split(invert(upper_t[first, first].T))
-    bottom = split(invert(upper_t[second, second].T))
+        for g in range(4):
+            upper_t[pl.ds(h * NB + g, 64, stride=4), :] = wide[h * NB + 64 * g : h * NB + 64 * g + 64, :]
+    corner = split(upper_t[NB : NB + HALF, :].T)
+    top = split(invert(upper_t[0:HALF, :].T))
+    bottom = split(invert(upper_t[NB + HALF : 2 * NB, :].T))
 
     def pivot_half(h):
         return jnp.concatenate([gathered[c, 8 * h : 8 * h + 8, 0].reshape(HALF, HALF) for c in range(2)], axis=1)
@@ -281,19 +282,23 @@
     upper = jnp.concatenate([upper_first, upper_second], axis=0)
     upper_parts = split(upper)
 
+    for place in (5, 7, 8):
+        ring_pass(place)
+    split_blocks(5, -5, 7, -7, 8)
+
     def store(n):
         part = pl.ds(n * CHUNK, CHUNK)
         return pltpu.make_async_copy(rows.at[part], out.at[part], store_sem.at[n])
 
     for n in range(ROWS // CHUNK):
         part = slice(n * CHUNK, (n + 1) * CHUNK)
-        value = rows[part, :] - dot3((panel_high[part, :], panel_low[part, :]), upper_parts)
+        value = rows[part, :] - dot3((panel_high[:, part], panel_low[:, part]), upper_parts, 0)
         if n == 0:
             value = jnp.where(is_root, upper, value)
         rows[part, :] = value
         store(n).start()
 
-    for copy in (sib_p, sib_g, sib_d, rs_all, ag_all, c_all, near_all, far_all):
+    for copy in (sib_p, sib_g, rs_all, ag_all, b_all, c_all):
         copy.wait_send()
     for place in range(1, LAST + 1):
         for d, h in ring_legs:
@@ -313,12 +318,12 @@
     return high, (a - high.astype(F32)).astype(BF16)
 
 
-def dot1(a, b):
-    return jnp.dot(a, b, preferred_element_type=F32)
-
-
-def dot3(a, b):
-    return dot1(a[0], b[0]) + (dot1(a[0], b[1]) + dot1(a[1], b[0]))
+def dot1(a, b, dim=1):
+    return lax.dot_general(a, b, (((dim,), (0,)), ((), ())), preferred_element_type=F32)
+
+
+def dot3(a, b, dim=1):
+    return dot1(a[0], b[0], dim) + (dot1(a[0], b[1], dim) + dot1(a[1], b[0], dim))
 
 
 def invert(square):
@@ -357,22 +362,22 @@
         scratch_shapes=[
             pltpu.VMEM((NZ, WIDTH, ROWS), F32),
             pltpu.VMEM((2, CHIPS, 2, 16, HALF), F32),
-            pltpu.VMEM((2, NB, HALF), F32),
+            pltpu.VMEM((2 * NB, HALF), F32),
             pltpu.SMEM((NB,), jnp.int32),
             pltpu.VMEM((1, NB), jnp.int32),
-            pltpu.VMEM((NB, NB), F32),
+            pltpu.VMEM((2 * NB, HALF), F32),
             pltpu.VMEM((NB, COLS), F32),
-            pltpu.VMEM((ROWS, NB), BF16),
-            pltpu.VMEM((ROWS, NB), BF16),
+            pltpu.VMEM((NB, ROWS), BF16),
+            pltpu.VMEM((NB, ROWS), BF16),
             pltpu.VMEM((ROWS, COLS), F32),
             pltpu.VMEM((3, NB, HALF), F32),
             pltpu.VMEM((NB, HALF), F32),
             pltpu.VMEM((CHIPS, 16, HALF), F32),
             pltpu.VMEM((2, 16, HALF), F32),
             pltpu.VMEM((16, HALF), F32),
-            pltpu.VMEM((2 * CHIPS, 1, HALF), F32),
-            pltpu.VMEM((NZ, 1, HALF), F32),
-            pltpu.VMEM((NZ, HALF), F32),
+            pltpu.VMEM((8, 4, HALF), F32),
+            pltpu.VMEM((NZ, 4, HALF), F32),
+            pltpu.VMEM((4 * NZ, HALF), F32),
             dma((4,)),
             dma((2, LAST + 1, 2)), dma((2, LAST + 1, 2)),
             dma, dma,
@@ -383,8 +388,8 @@
             dma, dma,
             dma, dma,
             dma, dma,
-            dma((2,)), dma((2,)),
             dma((ROWS // CHUNK,)),
+            pltpu.SemaphoreType.REGULAR,
         ],
         compiler_params=pltpu.CompilerParams(
             collective_id=0, has_side_effects=True, vmem_limit_bytes=63 * 1000 * 1024

time: 43.1 us -> 41.1 us (0.954)
  Pallas kernels: 40.7 us -> 38.7 us
    pallas_call x1, Pallas kernels: 40.7 us -> 38.7 us  [local(): pl.pallas_call(exchange_kernel, name='exchange', out_shape=jax.ShapeDtype...]
where the time goes in v4:
time: 41.1 us; the launch traced here: 41 us
  Pallas kernels  38.7 us (94%)
  local copies, waits for them, and re-layouts  2.26 us (5%)
    pallas_call x1, Pallas kernels, local(): pl.pallas_call(exchange_kernel, name='exchange', out_shape=jax.ShapeDtype...  38.7 us
    unnamed x1, local copies, waits for them, and re-layouts  2.26 us

profile of v4, /device:TPU:1, one launch (start us, length us, event | category | flops | bytes accessed | tf_op | source)
XLA Modules:
  0.0 41.0 jit_solution(6148242203486513263)
XLA Ops:
  0.0 38.7 %exchange.1 = f32[1024,256]{1,0:T(8,128)} custom-call(s32[256]{0:T(256)} %pivots.1, s32[1,256]{1,0:T(1,128)} %bitcast.3, f32[1024,256]{1,0:T(8,128)} %slab.1, f32[16,1024]{1,0:T(8,128)} %bitcast.2), custom_call_target="tpu_custom_call" | custom-call | tf_op jit(solution)/shard_map/exchange/pallas_call | solution.py:356
  38.7 2.3 %copy.5 = f32[1024,256]{1,0:T(8,128)} copy(f32[1024,256]{1,0:T(8,128)} %exchange.1) | data formatting | bytes 2097152

commit v5 on v4

--- a/solution.py
+++ b/solution.py
@@ -25,7 +25,7 @@
     pivots, pivot_row, slab, panel, out,
     pt, gathered, wide, piv, pivot_lanes, upper_t, leading, panel_high, panel_low, rows, masked, from_sibling, landed, mine, lead_in, piece, piece_in, column,
     local_sem, ring_send, ring_recv, a_send, a_recv, b_send, b_recv, c_send, c_recv,
-    lead_send, lead_recv, p_send, p_recv, rs_send, rs_recv, ag_send, ag_recv, g_send, g_recv, store_sem, known,
+    lead_send, lead_recv, p_send, p_recv, rs_send, rs_recv, ag_send, ag_recv, g_send, g_recv, known,
 ):
     p = lax.axis_index("prow")
     z = lax.axis_index("pcol")
@@ -69,15 +69,18 @@
     panel_copy = pltpu.make_async_copy(panel, pt.at[z], local_sem.at[0])
     slab_copy = pltpu.make_async_copy(slab, rows, local_sem.at[1])
     lanes_copy = pltpu.make_async_copy(pivot_row, pivot_lanes, local_sem.at[3])
+    panel_copy.start()
+    slab_copy.start()
     pivot_copy.start()
     lanes_copy.start()
-    panel_copy.start()
-    slab_copy.start()
-
-    for o in range(1, REACH + 1):
+
+    for o in (10, 9, 11, 6, 14):
+        greet((near(o), z))
+    for o in range(REACH, 0, -1):
         greet((p, above(o)))
         greet((p, above(-o)))
-    loop(1, CHIPS, lambda o: greet((near(o), z)))
+    for o in (2, 5, 7, 8, 13, 15, 1, 3, 4, 12):
+        greet((near(o), z))
     for other, c in square[1::2]:
         greet((2 * other + c, z))
     greet((sibling, z))
@@ -286,17 +289,12 @@
         ring_pass(place)
     split_blocks(5, -5, 7, -7, 8)
 
-    def store(n):
-        part = pl.ds(n * CHUNK, CHUNK)
-        return pltpu.make_async_copy(rows.at[part], out.at[part], store_sem.at[n])
-
     for n in range(ROWS // CHUNK):
         part = slice(n * CHUNK, (n + 1) * CHUNK)
         value = rows[part, :] - dot3((panel_high[:, part], panel_low[:, part]), upper_parts, 0)
         if n == 0:
             value = jnp.where(is_root, upper, value)
-        rows[part, :] = value
-        store(n).start()
+        out[part, :] = value
 
     for copy in (sib_p, sib_g, rs_all, ag_all, b_all, c_all):
         copy.wait_send()
@@ -308,9 +306,6 @@
     @pl.when(is_root)
     def _():
         a_all.wait_send()
-
-    for n in range(ROWS // CHUNK):
-        store(n).wait()
 
 
 def split(a):
@@ -358,7 +353,7 @@
         name="exchange",
         out_shape=jax.ShapeDtypeStruct((ROWS, COLS), F32),
         in_specs=[hbm] * 4,
-        out_specs=hbm,
+        out_specs=pl.BlockSpec(memory_space=pltpu.VMEM),
         scratch_shapes=[
             pltpu.VMEM((NZ, WIDTH, ROWS), F32),
             pltpu.VMEM((2, CHIPS, 2, 16, HALF), F32),
@@ -388,13 +383,12 @@
             dma, dma,
             dma, dma,
             dma, dma,
-            dma((ROWS // CHUNK,)),
             pltpu.SemaphoreType.REGULAR,
         ],
         compiler_params=pltpu.CompilerParams(
-            collective_id=0, has_side_effects=True, vmem_limit_bytes=63 * 1000 * 1024
+            collective_id=0, has_side_effects=True, vmem_limit_bytes=24576 * 1024
         ),
-    )(pivots, pivots.reshape(1, NB), slab, panel.T)
+    )(*(pltpu.with_memory_space_constraint(a, pltpu.HBM) for a in (pivots, pivots.reshape(1, NB), slab, panel.T)))
 
 
 def solution(mesh):

time: 41.1 us -> 39.1 us (0.951)
  local copies, waits for them, and re-layouts: 2.26 us -> 0.97 us
  Pallas kernels: 38.7 us -> 38 us
    unnamed x1, local copies, waits for them, and re-layouts: 2.26 us -> 0.97 us
    pallas_call x1, Pallas kernels: 38.7 us -> 38 us  [local(): pl.pallas_call(exchange_kernel, name='exchange', out_shape=jax.ShapeDtype...]
where the time goes in v5:
time: 39.1 us; the launch traced here: 39 us
  Pallas kernels  38 us (97%)
  local copies, waits for them, and re-layouts  0.97 us (2%)
    pallas_call x1, Pallas kernels, local(): pl.pallas_call(exchange_kernel, name='exchange', out_shape=jax.ShapeDtype...  38 us
    unnamed x1, local copies, waits for them, and re-layouts  0.97 us

profile of v5, /device:TPU:1, one launch (start us, length us, event | category | flops | bytes accessed | tf_op | source)
XLA Modules:
  0.0 39.0 jit_solution(17567230534291078166)
XLA Ops:
  0.0 38.0 %exchange.1 = f32[1024,256]{1,0:T(8,128)S(1)} custom-call(s32[256]{0:T(256)} %pivots.1, s32[1,256]{1,0:T(1,128)} %bitcast.3, f32[1024,256]{1,0:T(8,128)} %slab.1, f32[16,1024]{1,0:T(8,128)} %bitcast.2), custom_call_target="tpu_custom_call" | custom-call | tf_op jit(solution)/shard_map/exchange/pallas_call | solution.py:351
  38.0 1.0 %copy.5 = f32[1024,256]{1,0:T(8,128)} copy(f32[1024,256]{1,0:T(8,128)S(1)} %exchange.1) | data formatting | bytes 2097152

commit v6 on v5

--- a/solution.py
+++ b/solution.py
@@ -24,7 +24,7 @@
 def exchange_kernel(
     pivots, pivot_row, slab, panel, out,
     pt, gathered, wide, piv, pivot_lanes, upper_t, leading, panel_high, panel_low, rows, masked, from_sibling, landed, mine, lead_in, piece, piece_in, column,
-    local_sem, ring_send, ring_recv, a_send, a_recv, b_send, b_recv, c_send, c_recv,
+    local_sem, ring_send, ring_recv, leaf_recv, a_send, a_recv, b_send, b_recv, c_send, c_recv,
     lead_send, lead_recv, p_send, p_recv, rs_send, rs_recv, ag_send, ag_recv, g_send, g_recv, known,
 ):
     p = lax.axis_index("prow")
@@ -35,17 +35,17 @@
     is_root = p == 0
     outer = (core == 1) & (chip > 0)
 
-    def loop(first, last, act):
-        def body(o, carry):
-            act(o)
-            return carry
-        lax.fori_loop(first, last, body, 0)
+    def wrapped(index, size):
+        return jnp.where(index >= size, index - size, jnp.where(index < 0, index + size, index))
+
+    nears = [2 * wrapped(chip + o, CHIPS) + core for o in range(CHIPS)]
+    aboves = [wrapped(z + o, NZ) if o < 9 else wrapped(z + o - NZ, NZ) for o in range(NZ)]
 
     def near(o):
-        return 2 * lax.rem(chip + o, CHIPS) + core
+        return nears[o]
 
     def above(o):
-        return lax.rem(z + o + NZ, NZ)
+        return aboves[o % NZ]
 
     x, y = lax.div(chip, 4), lax.rem(chip, 4)
     x_odd, y_odd = lax.rem(x, 2), lax.rem(y, 2)
@@ -54,10 +54,9 @@
     square.append((chip, 1 - core))
 
     def part_of(target):
-        target_chip = lax.div(target, 2)
-        return 4 * lax.rem(lax.div(target_chip, 4), 2) + 2 * lax.rem(target_chip, 2) + lax.rem(target, 2)
-
-    mine_part = lax.div(part_of(p), 2)
+        return 4 * (target // 8 % 2) + 2 * (target // 2 % 2) + target % 2
+
+    mine_part = 2 * x_odd + y_odd
     relay = pl.ds(pl.multiple_of(core * NB + 64 * mine_part, 64), 64)
 
     barrier = pltpu.get_barrier_semaphore()
@@ -87,7 +86,8 @@
 
     @pl.when(is_root)
     def _():
-        loop(1, CHIPS, lambda o: greet((2 * o + 1, z)))
+        for o in range(1, CHIPS):
+            greet((2 * o + 1, z))
 
     @pl.when(outer)
     def _():
@@ -97,23 +97,6 @@
     for k in range(WIDTH):
         for h in range(2):
             piece[2 * (k % 4) + h, k // 4 : k // 4 + 1, :] = pt[z, k : k + 1, h * HALF : (h + 1) * HALF]
-    pivot_copy.wait()
-    lanes_copy.wait()
-    slab_copy.wait()
-
-    row_start = p * ROWS
-
-    def pick(k, carry):
-        local = piv[k] - row_start
-        held = (local >= 0) & (local < ROWS)
-        row = rows[pl.ds(jnp.clip(local, 0, ROWS - 1), 1), :]
-        row = jnp.where(held, row, 0.0)
-        masked[0, pl.ds(k, 1), :] = row[:, :HALF]
-        masked[1, pl.ds(k, 1), :] = row[:, HALF:]
-        return carry
-
-    lax.fori_loop(0, NB, pick, 0, unroll=8)
-
     greeted = 2 * REACH + CHIPS + 3
     pl.semaphore_wait(barrier, greeted + jnp.where(is_root, CHIPS - 1, jnp.where(outer, 1, 0)))
 
@@ -127,37 +110,41 @@
 
     def ring_copy(direction, place, half):
         jump = 2 - place % 2
-        part = pt.at[above(-direction * (place - jump)), pl.ds(8 * half, 8)]
+        block = above(-direction * (place - jump))
         d = (direction + 1) // 2
-        return remote(
-            part, part, ring_send.at[d, place, half], ring_recv.at[d, place, half], (p, above(direction * jump))
-        )
-
-    def ring_uses(direction, place, half):
-        return place < LAST or (place == LAST and half == (0 if direction == 1 else 1))
-
-    ring_legs = [(d, h) for h in range(2) for d in (1, -1)]
+        if place % 2:
+            part, arrived = pt.at[block], leaf_recv.at[place // 4]
+        else:
+            part = pt.at[block, pl.ds(8 * half, 8)]
+            arrived = leaf_recv.at[1] if place == LAST else ring_recv.at[d, place // 2 - 1, half]
+        return remote(part, part, ring_send, arrived, (p, above(direction * jump)))
 
     def ring_pass(place):
-        for d, h in ring_legs:
-            if place > 0 and ring_uses(d, place, h):
-                ring_copy(d, place, h).wait_recv()
-            if place % 2 == 0:
-                for later in (place + 2, place + 1):
-                    if ring_uses(d, later, h):
-                        ring_copy(d, later, h).start()
-
-    def a_copy(target):
-        return remote(piece.at[part_of(target)], piece_in.at[z], a_send, a_recv, (target, z))
-
-    def lead_copy(target):
-        t_chip, t_core = lax.div(target, 2), lax.rem(target, 2)
-        src = rows.at[pl.ds(t_chip * 16, 16), pl.ds(pl.multiple_of(t_core * HALF, HALF), HALF)]
+        for h in range(2):
+            for d in (1, -1):
+                if place > 0:
+                    ring_copy(d, place, h).wait_recv()
+                if place + 2 < LAST or h == (0 if d == 1 else 1):
+                    ring_copy(d, place + 2, h).start()
+        for d in (1, -1):
+            ring_copy(d, place + 1, 0).start()
+
+    def ring_leaves(group):
+        blocks = pt.at[pl.ds(0, 4 + group)]
+        remote(blocks, blocks, ring_send, leaf_recv.at[group], (p, z)).wait_recv()
+
+    ring_all = remote(pt.at[pl.ds(0, NZ - 1)], pt.at[pl.ds(0, NZ - 1)], ring_send, leaf_recv.at[0], (p, z))
+
+    def a_copy(target, part):
+        return remote(piece.at[part], piece_in.at[z], a_send, a_recv, (target, z))
+
+    def lead_copy(target, t_chip, t_core):
+        src = rows.at[pl.ds(t_chip * 16, 16), pl.ds(t_core * HALF, HALF)]
         return remote(src, lead_in, lead_send, lead_recv, (target, z))
 
     def rs_copy(o):
-        t_chip = lax.rem(chip + o, CHIPS)
-        return remote(masked.at[2, pl.ds(t_chip * 16, 16)], landed.at[o], rs_send, rs_recv, (near(o), z))
+        t_chip = wrapped(chip + o, CHIPS)
+        return remote(masked.at[2, pl.ds(pl.multiple_of(t_chip * 16, 16), 16)], landed.at[o], rs_send, rs_recv, (near(o), z))
 
     def ag_copy(o):
         return remote(mine, gathered.at[core, chip], ag_send, ag_recv, (near(o), z))
@@ -179,19 +166,21 @@
     def a_start():
         @pl.when(is_root)
         def _():
-            loop(1, 2 * CHIPS, lambda t: a_copy(t).start())
+            for t in sorted(range(1, 2 * CHIPS), key=lambda t: -(2 - abs(t // 8 - 2) - abs(t // 2 % 4 - 2))):
+                a_copy(t, part_of(t)).start()
             piece_in[z] = piece[0]
 
     def lead_start():
         @pl.when(is_root)
         def _():
-            loop(1, 2 * CHIPS, lambda t: lead_copy(t).start())
+            for t in range(1, 2 * CHIPS):
+                lead_copy(t, t // 2, t % 2).start()
             lead_in[...] = rows[0:16, 0:HALF]
 
     def b_start():
         @pl.when(p > 0)
         def _():
-            a_copy(p).wait_recv()
+            a_copy(0, 0).wait_recv()
         pl.semaphore_wait(known, 2)
         for o in (8, 7, 9, 6, 10, 5, 11, 4, 12, 3, 13, 2, 14, 1, 15):
             b_copy(o).start()
@@ -207,20 +196,22 @@
     def rs_start():
         sib_p.wait_recv()
         masked[2] = masked[core] + from_sibling[...]
-        loop(1, CHIPS, lambda o: rs_copy(o).start())
+        for o in range(1, CHIPS):
+            rs_copy(o).start()
 
     def ag_start():
         rs_all.wait_recv()
         @pl.when(p > 0)
         def _():
-            lead_copy(p).wait_recv()
+            lead_copy(0, 0, 0).wait_recv()
         total = masked[2, pl.ds(chip * 16, 16)]
         for o in range(1, CHIPS):
             total = total + landed[o]
         mine[0] = total
         mine[1] = lead_in[...]
         gathered[core, chip] = mine[...]
-        loop(1, CHIPS, lambda o: ag_copy(o).start())
+        for o in range(1, CHIPS):
+            ag_copy(o).start()
 
     def g_start():
         ag_all.wait_recv()
@@ -248,8 +239,25 @@
             panel_low[part, :] = low
 
     a_start()
+    ring_pass(0)
+    pivot_copy.wait()
+    lanes_copy.wait()
+    slab_copy.wait()
+
+    row_start = p * ROWS
+
+    def pick(k, carry):
+        local = piv[k] - row_start
+        held = (local >= 0) & (local < ROWS)
+        row = rows[pl.ds(jnp.clip(local, 0, ROWS - 1), 1), :]
+        row = jnp.where(held, row, 0.0)
+        masked[0, pl.ds(k, 1), :] = row[:, :HALF]
+        masked[1, pl.ds(k, 1), :] = row[:, HALF:]
+        return carry
+
+    lax.fori_loop(0, NB, pick, 0, unroll=8)
+
     sib_p.start()
-    ring_pass(0)
     lead_start()
     rs_start()
     b_start()
@@ -257,13 +265,12 @@
     split_blocks(0, 2, -2)
     ag_start()
     ring_pass(4)
-    ring_pass(1)
-    split_blocks(4, -4, 1, -1)
+    split_blocks(4, -4)
     c_start()
     ring_pass(6)
     g_start()
-    ring_pass(3)
-    split_blocks(3, -3, 6, -6)
+    ring_leaves(0)
+    split_blocks(1, -1, 3, -3, 6, -6)
     @pl.when(is_root)
     def _():
         lead_all.wait_send()
@@ -285,8 +292,7 @@
     upper = jnp.concatenate([upper_first, upper_second], axis=0)
     upper_parts = split(upper)
 
-    for place in (5, 7, 8):
-        ring_pass(place)
+    ring_leaves(1)
     split_blocks(5, -5, 7, -7, 8)
 
     for n in range(ROWS // CHUNK):
@@ -296,13 +302,8 @@
             value = jnp.where(is_root, upper, value)
         out[part, :] = value
 
-    for copy in (sib_p, sib_g, rs_all, ag_all, b_all, c_all):
+    for copy in (sib_p, sib_g, rs_all, ag_all, b_all, c_all, ring_all):
         copy.wait_send()
-    for place in range(1, LAST + 1):
-        for d, h in ring_legs:
-            if ring_uses(d, place, h):
-                ring_copy(d, place, h).wait_send()
-
     @pl.when(is_root)
     def _():
         a_all.wait_send()
@@ -374,7 +375,7 @@
             pltpu.VMEM((NZ, 4, HALF), F32),
             pltpu.VMEM((4 * NZ, HALF), F32),
             dma((4,)),
-            dma((2, LAST + 1, 2)), dma((2, LAST + 1, 2)),
+            dma, dma((2, 3, 2)), dma((2,)),
             dma, dma,
             dma, dma,
             dma, dma,

time: 39.1 us -> 37.1 us (0.949)
  Pallas kernels: 38 us -> 36 us
    pallas_call x1, Pallas kernels: 38 us -> 36 us  [local(): pl.pallas_call(exchange_kernel, name='exchange', out_shape=jax.ShapeDtype...]
where the time goes in v6:
time: 37.1 us; the launch traced here: 37 us
  Pallas kernels  36 us (97%)
  local copies, waits for them, and re-layouts  0.97 us (3%)
    pallas_call x1, Pallas kernels, local(): pl.pallas_call(exchange_kernel, name='exchange', out_shape=jax.ShapeDtype...  36 us
    unnamed x1, local copies, waits for them, and re-layouts  0.97 us

profile of v6, /device:TPU:1, one launch (start us, length us, event | category | flops | bytes accessed | tf_op | source)
XLA Modules:
  0.0 37.0 jit_solution(15841044156869016764)
XLA Ops:
  0.0 36.0 %exchange.1 = f32[1024,256]{1,0:T(8,128)S(1)} custom-call(s32[256]{0:T(256)} %pivots.1, s32[1,256]{1,0:T(1,128)} %bitcast.3, f32[1024,256]{1,0:T(8,128)} %slab.1, f32[16,1024]{1,0:T(8,128)} %bitcast.2), custom_call_target="tpu_custom_call" | custom-call | tf_op jit(solution)/shard_map/exchange/pallas_call | solution.py:352
  36.0 1.0 %copy.5 = f32[1024,256]{1,0:T(8,128)} copy(f32[1024,256]{1,0:T(8,128)S(1)} %exchange.1) | data formatting | bytes 2097152

commit v7 on v6

--- a/solution.py
+++ b/solution.py
@@ -16,16 +16,15 @@
 HALF = 128
 WIDTH = 16
 LAST = 8
-REACH = 4
 CHUNK = 256
 BASE = 32
 
 
 def exchange_kernel(
     pivots, pivot_row, slab, panel, out,
-    pt, gathered, wide, piv, pivot_lanes, upper_t, leading, panel_high, panel_low, rows, masked, from_sibling, landed, mine, lead_in, piece, piece_in, column,
-    local_sem, ring_send, ring_recv, leaf_recv, a_send, a_recv, b_send, b_recv, c_send, c_recv,
-    lead_send, lead_recv, p_send, p_recv, rs_send, rs_recv, ag_send, ag_recv, g_send, g_recv, known,
+    pt, gathered, wide, piv, pivot_lanes, upper_t, leading, panel_high, panel_low, rows, masked, from_sibling, landed, mine, lead_in, lead_rows, piece, piece_in, column,
+    local_sem, ring_send, ring_recv, leaf_recv, x_send, x_recv, a_send, a_recv, b_send, b_recv, c_send, c_recv,
+    lead_x_send, lead_x_recv, lead_send, lead_recv, p_send, p_recv, rs_send, rs_recv, ag_send, ag_recv, g_send, g_recv, line_known, near_known, far_known,
 ):
     p = lax.axis_index("prow")
     z = lax.axis_index("pcol")
@@ -33,7 +32,7 @@
     core = lax.rem(p, 2)
     sibling = 2 * chip + 1 - core
     is_root = p == 0
-    outer = (core == 1) & (chip > 0)
+    relays = lax.rem(p, 8) == 0
 
     def wrapped(index, size):
         return jnp.where(index >= size, index - size, jnp.where(index < 0, index + size, index))
@@ -52,9 +51,8 @@
     across, along = 4 - 8 * x_odd, 1 - 2 * y_odd
     square = [(chip + move, c) for move in (across + along, across, along) for c in (core, 1 - core)]
     square.append((chip, 1 - core))
-
-    def part_of(target):
-        return 4 * (target // 8 % 2) + 2 * (target // 2 % 2) + target % 2
+    lines = [2 * wrapped(chip + 4 * o, CHIPS) + core for o in (2, 1, 3)]
+    lines_y = [8 * x + 2 * jnp.where(y + o >= 4, y + o - 4, y + o) + core for o in (2, 1, 3)]
 
     mine_part = 2 * x_odd + y_odd
     relay = pl.ds(pl.multiple_of(core * NB + 64 * mine_part, 64), 64)
@@ -73,35 +71,41 @@
     pivot_copy.start()
     lanes_copy.start()
 
-    for o in (10, 9, 11, 6, 14):
-        greet((near(o), z))
-    for o in range(REACH, 0, -1):
+    for o in (2, 1):
         greet((p, above(o)))
         greet((p, above(-o)))
-    for o in (2, 5, 7, 8, 13, 15, 1, 3, 4, 12):
-        greet((near(o), z))
+    for device in lines + lines_y:
+        greet((device, z))
     for other, c in square[1::2]:
         greet((2 * other + c, z))
     greet((sibling, z))
 
+    @pl.when(relays)
+    def _():
+        for j in range(1, 4):
+            greet((8 * x + 2 * j + 1, z))
+
+    relayed_by_other = (core == 1) & (y > 0)
+
+    @pl.when(relayed_by_other)
+    def _():
+        greet((8 * x, z))
+
+    panel_copy.wait()
+
     @pl.when(is_root)
     def _():
-        for o in range(1, CHIPS):
-            greet((2 * o + 1, z))
-
-    @pl.when(outer)
-    def _():
-        greet((0, z))
-
-    panel_copy.wait()
-    for k in range(WIDTH):
-        for h in range(2):
-            piece[2 * (k % 4) + h, k // 4 : k // 4 + 1, :] = pt[z, k : k + 1, h * HALF : (h + 1) * HALF]
-    greeted = 2 * REACH + CHIPS + 3
-    pl.semaphore_wait(barrier, greeted + jnp.where(is_root, CHIPS - 1, jnp.where(outer, 1, 0)))
-
-    for o in (REACH, -REACH):
-        pl.semaphore_signal(known, inc=1, device_id=(p, above(o)), device_id_type=MESH)
+        for k in range(WIDTH):
+            for h in range(2):
+                piece[2 * (k % 4) + h, k // 4 : k // 4 + 1, :] = pt[z, k : k + 1, h * HALF : (h + 1) * HALF]
+
+    greeted = 4 + 6 + 3 + 1
+    pl.semaphore_wait(barrier, greeted + jnp.where(relays, 3, jnp.where(relayed_by_other, 1, 0)))
+
+    for device in lines:
+        pl.semaphore_signal(line_known, inc=1, device_id=(device, z), device_id_type=MESH)
+    for o in (2, -2):
+        pl.semaphore_signal(near_known, inc=1, device_id=(p, above(o)), device_id_type=MESH)
 
     def remote(src, dst, send, recv, device):
         return pltpu.make_async_remote_copy(
@@ -135,12 +139,22 @@
 
     ring_all = remote(pt.at[pl.ds(0, NZ - 1)], pt.at[pl.ds(0, NZ - 1)], ring_send, leaf_recv.at[0], (p, z))
 
-    def a_copy(target, part):
-        return remote(piece.at[part], piece_in.at[z], a_send, a_recv, (target, z))
-
-    def lead_copy(target, t_chip, t_core):
-        src = rows.at[pl.ds(t_chip * 16, 16), pl.ds(t_core * HALF, HALF)]
+    mine_first = pl.multiple_of(4 * x_odd, 4)
+
+    def x_copy(line):
+        return remote(piece.at[pl.ds(4 * (line % 2), 4)], piece.at[pl.ds(4 * (line % 2), 4)], x_send, x_recv, (8 * line, z))
+
+    def a_copy(target, j, c):
+        return remote(piece.at[mine_first + 2 * (j % 2) + c], piece_in.at[z], a_send, a_recv, (target, z))
+
+    def lead_x_copy(line):
+        return remote(rows.at[pl.ds(64 * line, 64)], lead_rows, lead_x_send, lead_x_recv, (8 * line, z))
+
+    def lead_copy(target, j, c):
+        src = lead_rows.at[pl.ds(16 * j, 16), pl.ds(c * HALF, HALF)]
         return remote(src, lead_in, lead_send, lead_recv, (target, z))
+
+    targets = [(8 * x + 2 * j + c, j, c) for j in (2, 1, 3) for c in range(2)] + [(8 * x + 1, 0, 1)]
 
     def rs_copy(o):
         t_chip = wrapped(chip + o, CHIPS)
@@ -160,29 +174,59 @@
     ag_all = remote(gathered.at[core, pl.ds(0, 15)], gathered.at[core, pl.ds(0, 15)], ag_send, ag_recv, here)
     c_all = remote(wide.at[pl.ds(0, 448)], wide.at[pl.ds(0, 448)], c_send, c_recv, here)
     b_all = remote(piece_in.at[pl.ds(0, 15)], piece_in.at[pl.ds(0, 15)], b_send, b_recv, here)
-    lead_all = remote(rows.at[pl.ds(0, 31 * 8)], rows.at[pl.ds(0, 31 * 8)], lead_send, lead_recv, here)
-    a_all = remote(masked.at[0, pl.ds(0, 124)], masked.at[0, pl.ds(0, 124)], a_send, a_recv, here)
+    x_all = remote(masked.at[0, pl.ds(0, 48)], masked.at[0, pl.ds(0, 48)], x_send, x_recv, here)
+    a_all = remote(masked.at[0, pl.ds(0, 28)], masked.at[0, pl.ds(0, 28)], a_send, a_recv, here)
+    lead_x_all = remote(rows.at[pl.ds(0, 192)], rows.at[pl.ds(0, 192)], lead_x_send, lead_x_recv, here)
+    lead_all = remote(masked.at[0, pl.ds(0, 112)], masked.at[0, pl.ds(0, 112)], lead_send, lead_recv, here)
+
+    def x_start():
+        @pl.when(is_root)
+        def _():
+            for line in (2, 1, 3):
+                x_copy(line).start()
+
+    def lead_x_start():
+        @pl.when(is_root)
+        def _():
+            for line in (2, 1, 3):
+                lead_x_copy(line).start()
+            lead_rows[...] = rows[0:64, :]
 
     def a_start():
-        @pl.when(is_root)
-        def _():
-            for t in sorted(range(1, 2 * CHIPS), key=lambda t: -(2 - abs(t // 8 - 2) - abs(t // 2 % 4 - 2))):
-                a_copy(t, part_of(t)).start()
-            piece_in[z] = piece[0]
+        @pl.when(relays)
+        def _():
+            @pl.when(p > 0)
+            def _():
+                x_copy(0).wait_recv()
+            for target in targets:
+                a_copy(*target).start()
+            piece_in[z] = piece[mine_first]
 
     def lead_start():
-        @pl.when(is_root)
-        def _():
-            for t in range(1, 2 * CHIPS):
-                lead_copy(t, t // 2, t % 2).start()
-            lead_in[...] = rows[0:16, 0:HALF]
+        @pl.when(relays)
+        def _():
+            @pl.when(p > 0)
+            def _():
+                lead_x_copy(0).wait_recv()
+            for target in targets:
+                lead_copy(*target).start()
+            lead_in[...] = lead_rows[0:16, 0:HALF]
+
+    def tell_column():
+        pl.semaphore_wait(near_known, 2)
+        for o in (4, -4):
+            pl.semaphore_signal(far_known, inc=1, device_id=(p, above(o)), device_id_type=MESH)
 
     def b_start():
-        @pl.when(p > 0)
-        def _():
-            a_copy(0, 0).wait_recv()
-        pl.semaphore_wait(known, 2)
-        for o in (8, 7, 9, 6, 10, 5, 11, 4, 12, 3, 13, 2, 14, 1, 15):
+        @pl.when(jnp.logical_not(relays))
+        def _():
+            a_copy(0, 0, 0).wait_recv()
+        for o in (4, 12, 3, 13, 2, 14, 1, 15):
+            b_copy(o).start()
+
+    def b_far_start():
+        pl.semaphore_wait(far_known, 2)
+        for o in (8, 7, 9, 6, 10, 5, 11):
             b_copy(o).start()
 
     def c_start():
@@ -196,12 +240,13 @@
     def rs_start():
         sib_p.wait_recv()
         masked[2] = masked[core] + from_sibling[...]
+        pl.semaphore_wait(line_known, 3)
         for o in range(1, CHIPS):
             rs_copy(o).start()
 
     def ag_start():
         rs_all.wait_recv()
-        @pl.when(p > 0)
+        @pl.when(jnp.logical_not(relays))
         def _():
             lead_copy(0, 0, 0).wait_recv()
         total = masked[2, pl.ds(chip * 16, 16)]
@@ -238,7 +283,7 @@
             panel_high[part, :] = high
             panel_low[part, :] = low
 
-    a_start()
+    x_start()
     ring_pass(0)
     pivot_copy.wait()
     lanes_copy.wait()
@@ -258,22 +303,27 @@
     lax.fori_loop(0, NB, pick, 0, unroll=8)
 
     sib_p.start()
+    lead_x_start()
+    a_start()
+    tell_column()
+    rs_start()
     lead_start()
-    rs_start()
+    ring_pass(2)
     b_start()
-    ring_pass(2)
     split_blocks(0, 2, -2)
+    b_far_start()
     ag_start()
     ring_pass(4)
     split_blocks(4, -4)
+    ring_leaves(0)
+    split_blocks(1, -1, 3, -3)
+    ring_pass(6)
     c_start()
-    ring_pass(6)
     g_start()
-    ring_leaves(0)
-    split_blocks(1, -1, 3, -3, 6, -6)
+    split_blocks(6, -6)
     @pl.when(is_root)
     def _():
-        lead_all.wait_send()
+        lead_x_all.wait_send()
     swap_rows()
     c_all.wait_recv()
 
@@ -304,9 +354,14 @@
 
     for copy in (sib_p, sib_g, rs_all, ag_all, b_all, c_all, ring_all):
         copy.wait_send()
+    @pl.when(relays)
+    def _():
+        a_all.wait_send()
+        lead_all.wait_send()
+
     @pl.when(is_root)
     def _():
-        a_all.wait_send()
+        x_all.wait_send()
 
 
 def split(a):
@@ -371,6 +426,7 @@
             pltpu.VMEM((CHIPS, 16, HALF), F32),
             pltpu.VMEM((2, 16, HALF), F32),
             pltpu.VMEM((16, HALF), F32),
+            pltpu.VMEM((64, COLS), F32),
             pltpu.VMEM((8, 4, HALF), F32),
             pltpu.VMEM((NZ, 4, HALF), F32),
             pltpu.VMEM((4 * NZ, HALF), F32),
@@ -384,6 +440,10 @@
             dma, dma,
             dma, dma,
             dma, dma,
+            dma, dma,
+            dma, dma,
+            pltpu.SemaphoreType.REGULAR,
+            pltpu.SemaphoreType.REGULAR,
             pltpu.SemaphoreType.REGULAR,
         ],
         compiler_params=pltpu.CompilerParams(

time: 37.1 us -> 40.1 us (1.081)
  Pallas kernels: 36 us -> 39 us
    pallas_call x1, Pallas kernels: 36 us -> 39 us  [local(): pl.pallas_call(exchange_kernel, name='exchange', out_shape=jax.ShapeDtype...]
where the time goes in v7:
time: 40.1 us; the launch traced here: 40 us
  Pallas kernels  39 us (97%)
  local copies, waits for them, and re-layouts  0.97 us (2%)
    pallas_call x1, Pallas kernels, local(): pl.pallas_call(exchange_kernel, name='exchange', out_shape=jax.ShapeDtype...  39 us
    unnamed x1, local copies, waits for them, and re-layouts  0.97 us

profile of v7, /device:TPU:1, one launch (start us, length us, event | category | flops | bytes accessed | tf_op | source)
XLA Modules:
  0.0 40.0 jit_solution(13937073580164172229)
XLA Ops:
  0.0 39.0 %exchange.1 = f32[1024,256]{1,0:T(8,128)S(1)} custom-call(s32[256]{0:T(256)} %pivots.1, s32[1,256]{1,0:T(1,128)} %bitcast.3, f32[1024,256]{1,0:T(8,128)} %slab.1, f32[16,1024]{1,0:T(8,128)} %bitcast.2), custom_call_target="tpu_custom_call" | custom-call | tf_op jit(solution)/shard_map/exchange/pallas_call | solution.py:407
  39.0 1.0 %copy.5 = f32[1024,256]{1,0:T(8,128)} copy(f32[1024,256]{1,0:T(8,128)S(1)} %exchange.1) | data formatting | bytes 2097152

commit v8 on v6

--- a/solution.py
+++ b/solution.py
@@ -16,6 +16,8 @@
 HALF = 128
 WIDTH = 16
 LAST = 8
+PARTS = 4
+LEAVES_AFTER = {0: (1,), 2: (3,), 4: (5,), 6: (7,)}
 REACH = 4
 CHUNK = 256
 BASE = 32
@@ -108,26 +110,32 @@
             src_ref=src, dst_ref=dst, send_sem=send, recv_sem=recv, device_id=device, device_id_type=MESH
         )
 
-    def ring_copy(direction, place, half):
+    def ring_copy(direction, place, piece_of):
         jump = 2 - place % 2
         block = above(-direction * (place - jump))
         d = (direction + 1) // 2
         if place % 2:
             part, arrived = pt.at[block], leaf_recv.at[place // 4]
         else:
-            part = pt.at[block, pl.ds(8 * half, 8)]
-            arrived = leaf_recv.at[1] if place == LAST else ring_recv.at[d, place // 2 - 1, half]
+            part = pt.at[block, pl.ds(8 * (2 * piece_of // PARTS), 8)]
+            if PARTS == 1:
+                part = pt.at[block]
+            elif PARTS > 2:
+                width = 2 * ROWS // PARTS
+                part = pt.at[block, pl.ds(8 * (2 * piece_of // PARTS), 8), pl.ds(width * (piece_of % (PARTS // 2)), width)]
+            arrived = leaf_recv.at[1] if place == LAST else ring_recv.at[d, place // 2 - 1, piece_of]
         return remote(part, part, ring_send, arrived, (p, above(direction * jump)))
 
     def ring_pass(place):
-        for h in range(2):
+        for q in range(PARTS):
             for d in (1, -1):
                 if place > 0:
-                    ring_copy(d, place, h).wait_recv()
-                if place + 2 < LAST or h == (0 if d == 1 else 1):
-                    ring_copy(d, place + 2, h).start()
-        for d in (1, -1):
-            ring_copy(d, place + 1, 0).start()
+                    ring_copy(d, place, q).wait_recv()
+                if place + 2 < LAST or (2 * q < PARTS) == (d == 1):
+                    ring_copy(d, place + 2, q).start()
+        for leaf in LEAVES_AFTER[place]:
+            for d in (1, -1):
+                ring_copy(d, leaf, 0).start()
 
     def ring_leaves(group):
         blocks = pt.at[pl.ds(0, 4 + group)]
@@ -218,7 +226,6 @@
         sib_g.start()
 
     def swap_rows():
-        sib_g.wait_recv()
         for h in range(2):
             leading[:, h * HALF : (h + 1) * HALF] = gathered[h, :, 1].reshape(NB, HALF)
         lead_high, lead_low = split(leading[...])
@@ -274,7 +281,6 @@
     @pl.when(is_root)
     def _():
         lead_all.wait_send()
-    swap_rows()
     c_all.wait_recv()
 
     for h in range(2):
@@ -287,10 +293,12 @@
     def pivot_half(h):
         return jnp.concatenate([gathered[c, 8 * h : 8 * h + 8, 0].reshape(HALF, HALF) for c in range(2)], axis=1)
 
+    sib_g.wait_recv()
     upper_first = dot3(top, split(pivot_half(0)))
     upper_second = dot3(bottom, split(pivot_half(1) - dot3(corner, split(upper_first))))
     upper = jnp.concatenate([upper_first, upper_second], axis=0)
     upper_parts = split(upper)
+    swap_rows()
 
     ring_leaves(1)
     split_blocks(5, -5, 7, -7, 8)
@@ -375,7 +383,7 @@
             pltpu.VMEM((NZ, 4, HALF), F32),
             pltpu.VMEM((4 * NZ, HALF), F32),
             dma((4,)),
-            dma, dma((2, 3, 2)), dma((2,)),
+            dma, dma((2, 3, 4)), dma((2,)),
             dma, dma,
             dma, dma,
             dma, dma,

time: 37.1 us -> 35.7 us (0.962)
  Pallas kernels: 36 us -> 34.6 us
    pallas_call x1, Pallas kernels: 36 us -> 34.6 us  [local(): pl.pallas_call(exchange_kernel, name='exchange', out_shape=jax.ShapeDtype...]
where the time goes in v8:
time: 35.7 us; the launch traced here: 35.6 us
  Pallas kernels  34.6 us (97%)
  local copies, waits for them, and re-layouts  0.97 us (3%)
    pallas_call x1, Pallas kernels, local(): pl.pallas_call(exchange_kernel, name='exchange', out_shape=jax.ShapeDtype...  34.6 us
    unnamed x1, local copies, waits for them, and re-layouts  0.97 us

profile of v8, /device:TPU:1, one launch (start us, length us, event | category | flops | bytes accessed | tf_op | source)
XLA Modules:
  0.0 35.6 jit_solution(10151862127124047848)
XLA Ops:
  0.0 34.6 %exchange.1 = f32[1024,256]{1,0:T(8,128)S(1)} custom-call(s32[256]{0:T(256)} %pivots.1, s32[1,256]{1,0:T(1,128)} %bitcast.3, f32[1024,256]{1,0:T(8,128)} %slab.1, f32[16,1024]{1,0:T(8,128)} %bitcast.2), custom_call_target="tpu_custom_call" | custom-call | tf_op jit(solution)/shard_map/exchange/pallas_call | solution.py:360
  34.6 1.0 %copy.5 = f32[1024,256]{1,0:T(8,128)} copy(f32[1024,256]{1,0:T(8,128)S(1)} %exchange.1) | data formatting | bytes 2097152

commit v9 on v8

--- a/solution.py
+++ b/solution.py
@@ -16,6 +16,7 @@
 HALF = 128
 WIDTH = 16
 LAST = 8
+LATE = (5, -5, 7, -7, 8)
 PARTS = 4
 LEAVES_AFTER = {0: (1,), 2: (3,), 4: (5,), 6: (7,)}
 REACH = 4
@@ -25,7 +26,7 @@
 
 def exchange_kernel(
     pivots, pivot_row, slab, panel, out,
-    pt, gathered, wide, piv, pivot_lanes, upper_t, leading, panel_high, panel_low, rows, masked, from_sibling, landed, mine, lead_in, piece, piece_in, column,
+    pt, gathered, wide, piv, pivot_lanes, upper_t, leading, panel_high, panel_low, upper_high, upper_low, late_panel, late_upper, rows, masked, from_sibling, landed, mine, lead_in, piece, piece_in, column,
     local_sem, ring_send, ring_recv, leaf_recv, a_send, a_recv, b_send, b_recv, c_send, c_recv,
     lead_send, lead_recv, p_send, p_recv, rs_send, rs_recv, ag_send, ag_recv, g_send, g_recv, known,
 ):
@@ -237,13 +238,14 @@
             part = slice(n * CHUNK, (n + 1) * CHUNK)
             rows[part, :] = jnp.where(dot1(chosen, ones) > 0.5, replaced, rows[part, :])
 
+    def block_rows(place):
+        return pl.ds(pl.multiple_of(WIDTH * above(place), WIDTH), WIDTH)
+
     def split_blocks(*places):
         for place in places:
-            block = above(place)
-            high, low = split(pt[block])
-            part = pl.ds(pl.multiple_of(WIDTH * block, WIDTH), WIDTH)
-            panel_high[part, :] = high
-            panel_low[part, :] = low
+            high, low = split(pt[above(place)])
+            panel_high[block_rows(place), :] = high
+            panel_low[block_rows(place), :] = low
 
     a_start()
     ring_pass(0)
@@ -298,14 +300,32 @@
     upper_second = dot3(bottom, split(pivot_half(1) - dot3(corner, split(upper_first))))
     upper = jnp.concatenate([upper_first, upper_second], axis=0)
     upper_parts = split(upper)
+    upper_high[...], upper_low[...] = upper_parts
     swap_rows()
 
-    ring_leaves(1)
-    split_blocks(5, -5, 7, -7, 8)
-
+    for place in LATE:
+        for ref in (panel_high, panel_low):
+            ref[block_rows(place), :] = jnp.zeros((WIDTH, ROWS), BF16)
     for n in range(ROWS // CHUNK):
         part = slice(n * CHUNK, (n + 1) * CHUNK)
-        value = rows[part, :] - dot3((panel_high[:, part], panel_low[:, part]), upper_parts, 0)
+        rows[part, :] -= dot3((panel_high[:, part], panel_low[:, part]), upper_parts, 0)
+
+    count = len(LATE) * WIDTH
+    late_panel[3 * count :, :] = jnp.zeros((NB - 3 * count, ROWS), BF16)
+    late_upper[3 * count :, :] = jnp.zeros((NB - 3 * count, COLS), BF16)
+    for i, place in enumerate(LATE):
+        for term, ref in enumerate((upper_high, upper_low, upper_high)):
+            late_upper[term * count + i * WIDTH : term * count + (i + 1) * WIDTH, :] = ref[block_rows(place), :]
+
+    ring_leaves(1)
+    for i, place in enumerate(LATE):
+        high, low = split(pt[above(place)])
+        for term, value in enumerate((high, high, low)):
+            late_panel[term * count + i * WIDTH : term * count + (i + 1) * WIDTH, :] = value
+
+    for n in range(ROWS // CHUNK):
+        part = slice(n * CHUNK, (n + 1) * CHUNK)
+        value = rows[part, :] - dot1(late_panel[:, part], late_upper[...], 0)
         if n == 0:
             value = jnp.where(is_root, upper, value)
         out[part, :] = value
@@ -373,6 +393,10 @@
             pltpu.VMEM((NB, COLS), F32),
             pltpu.VMEM((NB, ROWS), BF16),
             pltpu.VMEM((NB, ROWS), BF16),
+            pltpu.VMEM((NB, COLS), BF16),
+            pltpu.VMEM((NB, COLS), BF16),
+            pltpu.VMEM((NB, ROWS), BF16),
+            pltpu.VMEM((NB, COLS), BF16),
             pltpu.VMEM((ROWS, COLS), F32),
             pltpu.VMEM((3, NB, HALF), F32),
             pltpu.VMEM((NB, HALF), F32),

time: 35.7 us -> 35.7 us (level)
  no operation moved by 1% of the time
where the time goes in v9:
time: 35.7 us; the launch traced here: 35.6 us
  Pallas kernels  34.6 us (97%)
  local copies, waits for them, and re-layouts  0.97 us (3%)
    pallas_call x1, Pallas kernels, local(): pl.pallas_call(exchange_kernel, name='exchange', out_shape=jax.ShapeDtype...  34.6 us
    unnamed x1, local copies, waits for them, and re-layouts  0.97 us

profile of v9, /device:TPU:1, one launch (start us, length us, event | category | flops | bytes accessed | tf_op | source)
XLA Modules:
  0.0 35.6 jit_solution(1150400425921927001)
XLA Ops:
  0.0 34.6 %exchange.1 = f32[1024,256]{1,0:T(8,128)S(1)} custom-call(s32[256]{0:T(256)} %pivots.1, s32[1,256]{1,0:T(1,128)} %bitcast.3, f32[1024,256]{1,0:T(8,128)} %slab.1, f32[16,1024]{1,0:T(8,128)} %bitcast.2), custom_call_target="tpu_custom_call" | custom-call | tf_op jit(solution)/shard_map/exchange/pallas_call | solution.py:380
  34.6 1.0 %copy.5 = f32[1024,256]{1,0:T(8,128)} copy(f32[1024,256]{1,0:T(8,128)S(1)} %exchange.1) | data formatting | bytes 2097152
